TPU v7x, 32 devices: a whole 2x2x4 slice. The times are simulated.
32 devices in a mesh: pw: 8 (over z, y), band: 4 (over x, core).
Axes of the slice: x: 2, y: 2, z: 4, core: 2. Of those that a mesh axis runs over, the one named last changes fastest.
Arguments:
- residual_directions: float32 [2, 512, 4, 2048], P(None, 'pw', 'band'), may hold values from -6 to 6
- local_field_applied: float32 [2, 512, 4, 2048], P(None, 'pw', 'band'), may hold values from -6 to 6
- orbital_running_sum: bfloat16 [2, 2048, 4, 2048], P(None, None, 'band', 'pw'), may hold values from -6 to 6
- energy_operator_running_sum: bfloat16 [2, 2048, 4, 2048], P(None, None, 'band', 'pw'), may hold values from -6 to 6
- coefficient_store: bfloat16 [4, 512, 2048], P('band'), may hold values from -0.25 to 0.25
- slab_keepers: int32 [2], replicated, may hold values from 0 to 3
- lattice_position: int32 [4, 2048], P('band', 'pw'), may hold values from 0 to 262143
Outputs:
- psi_new: bfloat16 [2, 2048, 4, 2048], P(None, None, 'band', 'pw')
- hpsi_new: bfloat16 [2, 2048, 4, 2048], P(None, None, 'band', 'pw')
Inputs may be any that keep to these rules, and one draw needn't show every extreme that they name: `slab_keepers`: each panel's owner is an index along band. `lattice_position`: grid points are row-major indices of a 64 x 64 x 64 grid, not necessarily distinct.
All inputs are finite; a program needn't handle non-finite values.
Results may differ from a plain program's by a relative error of at most 0.001.
Values may be sent and summed in bfloat16 or wider, within the bound.
A program may use at most 128 MiB of HBM per device.

v0:
```python
import jax
import jax.numpy as jnp
from jax import lax
from jax.sharding import PartitionSpec as P

RESIDUAL_NUMBER = 512
SLAB_LENGTH = 256
GRID = 64


def from_root(value, axis, source):
    kept = jnp.where(lax.axis_index(axis) == source, value, 0).astype(value.dtype)
    return lax.psum(kept, axis)


def kinetic_of(lattice_position):
    first = lattice_position // (GRID * GRID)
    second = lattice_position // GRID % GRID
    third = lattice_position % GRID
    total = jnp.zeros(lattice_position.shape, jnp.int32)
    for index in (first, second, third):
        folded = jnp.where(index >= GRID // 2, index - GRID, index)
        total = total + folded * folded
    return total.astype(jnp.float32) / (GRID * GRID)


def rotate_plane(panels, plane):
    total = None
    for subspace_slab in range(len(panels)):
        block = plane[subspace_slab * SLAB_LENGTH : (subspace_slab + 1) * SLAB_LENGTH]
        term = lax.dot_general(
            panels[subspace_slab],
            block,
            (((0,), (0,)), ((), ())),
            precision=lax.Precision.HIGHEST,
            preferred_element_type=jnp.float32,
        )
        total = term if total is None else total + term
    return total


def per_device(
    residual_directions,
    local_field_applied,
    orbital_running_sum,
    energy_operator_running_sum,
    coefficient_store,
    slab_keepers,
    lattice_position,
):
    count = RESIDUAL_NUMBER // SLAB_LENGTH
    panels = []
    for subspace_slab in range(count):
        slab_piece = coefficient_store[
            0, subspace_slab * SLAB_LENGTH : (subspace_slab + 1) * SLAB_LENGTH
        ]
        panels.append(
            from_root(slab_piece, "band", slab_keepers[subspace_slab]).astype(jnp.float32)
        )
    outgoing = (residual_directions, local_field_applied)
    local_kinetic = kinetic_of(lattice_position)
    corr_part = lax.all_to_all(outgoing[0], "pw", split_axis=3, concat_axis=1, tiled=True)
    second_part = lax.all_to_all(outgoing[1], "pw", split_axis=3, concat_axis=1, tiled=True)
    planes_count = corr_part.shape[0]
    rows = corr_part.shape[1]
    width = corr_part.shape[3]
    corr_flat = corr_part.reshape(planes_count, rows, width)
    second_flat = second_part.reshape(planes_count, rows, width)
    hcorr_flat = local_kinetic.reshape(1, 1, width) * corr_flat + second_flat
    psi_planes = [
        rotate_plane(panels, corr_flat[plane_index]) for plane_index in range(planes_count)
    ]
    hpsi_planes = [
        rotate_plane(panels, hcorr_flat[plane_index]) for plane_index in range(planes_count)
    ]
    span = psi_planes[0].shape[0]
    psi_stack = jnp.stack(psi_planes, axis=0).reshape(planes_count, span, 1, width)
    hpsi_stack = jnp.stack(hpsi_planes, axis=0).reshape(planes_count, span, 1, width)
    psi_new = (orbital_running_sum.astype(jnp.float32) + psi_stack).astype(jnp.bfloat16)
    hpsi_new = (energy_operator_running_sum.astype(jnp.float32) + hpsi_stack).astype(jnp.bfloat16)
    return (psi_new, hpsi_new)


def solution(mesh):
    in_specs = (
        P(None, "pw", "band", None),
        P(None, "pw", "band", None),
        P(None, None, "band", "pw"),
        P(None, None, "band", "pw"),
        P("band", None, None),
        P(),
        P("band", "pw"),
    )
    out_specs = (P(None, None, "band", "pw"), P(None, None, "band", "pw"))
    return jax.shard_map(
        per_device, mesh=mesh, in_specs=in_specs, out_specs=out_specs, check_vma=False
    )
```

profile of v0, /device:TPU:0, one launch (start us, length us, event | category | flops | bytes accessed | tf_op | source)
XLA Modules:
  0.0 130.7 jit_solution(16317375907731459070)
XLA Ops:
  7.2 4.1 %copy.42 = f32[2,64,1,2048]{1,0,2,3:T(2,128)S(1)} copy(f32[2,64,1,2048]{3,2,1,0:T(1,128)} %param.7) | data formatting | bytes 2097152 | tf_op args[0]
  11.3 3.0 %reshape.42 = f32[8,1,32768]{2,1,0:T(1,128)} reshape(f32[2048,1,2,64]{3,2,1,0:T(2,128)S(1)} %bitcast.84) | data formatting | bytes 2097152
  14.3 7.3 %all-to-all-start = ((f32[8,1,32768]{2,1,0:T(1,128)}), f32[8,1,32768]{2,1,0:T(1,128)S(1)}, u32[]{:S(2)}, u32[]{:S(2)}) async-start(f32[8,1,32768]{2,1,0:T(1,128)} %reshape.42), calls=%async_computation | async-start | bytes 2097152 | tf_op jit(solution)/shard_map/all_to_all | solution.py:62
  21.6 4.1 %copy.50 = f32[2,64,1,2048]{1,0,2,3:T(2,128)S(1)} copy(f32[2,64,1,2048]{3,2,1,0:T(1,128)} %param.8) | data formatting | bytes 2097152 | tf_op args[1]
  25.7 0.0 copy-start.9
  25.7 3.0 %reshape.44 = f32[8,1,32768]{2,1,0:T(1,128)} reshape(f32[2048,1,2,64]{3,2,1,0:T(2,128)S(1)} %bitcast.85) | data formatting | bytes 2097152
  28.7 0.0 copy-start.6
  28.7 18.6 %all-to-all-done = f32[8,1,32768]{2,1,0:T(1,128)S(1)} async-done(((f32[8,1,32768]{2,1,0:T(1,128)}), f32[8,1,32768]{2,1,0:T(1,128)S(1)}, u32[]{:S(2)}, u32[]{:S(2)}) %all-to-all-start) | async-done | bytes 1048608 | tf_op jit(solution)/shard_map/all_to_all | solution.py:62
  47.3 0.0 copy-start.4
  47.3 4.2 %all-to-all-start.1 = ((f32[8,1,32768]{2,1,0:T(1,128)}), f32[8,1,32768]{2,1,0:T(1,128)}, u32[]{:S(2)}, u32[]{:S(2)}) async-start(f32[8,1,32768]{2,1,0:T(1,128)} %reshape.44), calls=%async_computation.1 | async-start | bytes 2097152 | tf_op jit(solution)/shard_map/all_to_all | solution.py:63
  51.6 0.2 all-reduce.3.cloned.1.call-start
  51.8 0.0 copy-done.9
  51.8 0.6 fusion.19
  53.7 0.0 copy-done.6
  53.7 1.5 %select_bitcast_fusion = (bf16[256,2048]{1,0:T(8,128)(2,1)}, bf16[256,2048]{1,0:T(8,128)(2,1)}) fusion(bf16[1,512,2048]{2,1,0:T(8,128)(2,1)S(1)} %copy-done.6, pred[]{:T(512)S(6)} %eq.10, pred[]{:T(512)S(6)} %eq.9), kind=kLoop, calls=%fused_computation.17 | loop fusion | flops 1048576 | bytes 4194306 | tf_op jit(solution)/shard_map/jit(_where)/select_n | solution.py:12
  55.2 0.0 copy-done.4
  55.2 0.0 copy-start.10
  55.2 0.0 copy-start.5
  55.2 0.0 all-reduce.3.cloned.1.call-update
  55.2 0.7 copy-done.10
  55.9 0.5 broadcast.42
  56.4 0.0 copy-done.5
  56.4 3.1 %reduce.1 = f32[8,32768]{1,0:T(8,128)S(1)} reduce(f32[8,1,32768]{2,1,0:T(1,128)S(1)} %copy-done.5, f32[]{:T(128)} %broadcast.42), dimensions={1}, to_apply=%all_to_all.22.reduce_sub_computation | reduce | bytes 2097156 | tf_op jit(solution)/shard_map/all_to_all | solution.py:62
  59.6 1.5 %reshape.43 = f32[2048,1,2,64]{3,2,1,0:T(2,128)S(1)} reshape(f32[8,32768]{1,0:T(8,128)S(1)} %reduce.1) | data formatting | bytes 2097152
  61.1 2.1 %copy.56 = f32[2,64,1,8,256]{4,1,3,0,2:T(8,128)} copy(f32[2,64,1,8,256]{1,0,4,3,2:T(2,128)S(1)} %bitcast.81) | data formatting | bytes 2097152 | tf_op jit(solution)/shard_map/all_to_all | solution.py:62
  63.2 1.6 %copy.55 = f32[2,64,1,8,256]{4,3,1,0,2:T(8,128)} copy(f32[2,64,1,8,256]{1,0,4,3,2:T(2,128)S(1)} %bitcast.82) | data formatting | bytes 2097152 | tf_op jit(solution)/shard_map/all_to_all | solution.py:62
  64.8 12.4 %all-to-all-done.1 = f32[8,1,32768]{2,1,0:T(1,128)} async-done(((f32[8,1,32768]{2,1,0:T(1,128)}), f32[8,1,32768]{2,1,0:T(1,128)}, u32[]{:S(2)}, u32[]{:S(2)}) %all-to-all-start.1) | async-done | bytes 1048608 | tf_op jit(solution)/shard_map/all_to_all | solution.py:63
  77.2 4.4 %reduce = f32[8,32768]{1,0:T(8,128)S(1)} reduce(f32[8,1,32768]{2,1,0:T(1,128)} %all-to-all-done.1, f32[]{:T(128)} %broadcast.42), dimensions={1}, to_apply=%all_to_all.25.reduce_sub_computation | reduce | bytes 2097156 | tf_op jit(solution)/shard_map/all_to_all | solution.py:63
  81.5 1.5 %reshape.45 = f32[2048,1,2,64]{3,2,1,0:T(2,128)S(1)} reshape(f32[8,32768]{1,0:T(8,128)S(1)} %reduce) | data formatting | bytes 2097152
  83.1 0.0 copy-start.3
  83.1 2.1 %copy.58 = f32[2,64,1,8,256]{4,1,3,0,2:T(8,128)} copy(f32[2,64,1,8,256]{1,0,4,3,2:T(2,128)S(1)} %bitcast.83) | data formatting | bytes 2097152 | tf_op jit(solution)/shard_map/all_to_all | solution.py:63
  85.2 0.0 copy-done.3
  85.2 1.4 %multiply_add_fusion = f32[2,512,256]{2,1,0:T(8,128)S(1)} fusion(f32[2,512,256]{2,1,0:T(8,128)} %bitcast.88, f32[2,512,256]{2,1,0:T(8,128)S(1)} %bitcast.87, f32[256]{0:T(256)S(1)} %bitcast.93), kind=kLoop, calls=%fused_computation.16 | loop fusion | flops 524288 | bytes 3146752 | tf_op jit(solution)/shard_map/add | solution.py:69
  86.5 21.8 %all-reduce.3.cloned.1.call-done = (bf16[256,2048]{1,0:T(8,128)(2,1)}, bf16[256,2048]{1,0:T(8,128)(2,1)}) async-done(((bf16[256,2048]{1,0:T(8,128)(2,1)}, bf16[256,2048]{1,0:T(8,128)(2,1)}), (bf16[256,2048]{1,0:T(8,128)(2,1)}, bf16[256,2048]{1,0:T(8,128)(2,1)})) %all-reduce.3.cloned.1.call-update) | async-done | bytes 2097168 | tf_op jit(solution)/shard_map/psum | solution.py:13
  108.4 0.0 copy-start
  108.4 2.6 %fusion.10 = f32[2048,256]{1,0:T(8,128)S(1)} fusion(bf16[256,2048]{1,0:T(8,128)(2,1)} %get-tuple-element.12, f32[2,512,256]{2,1,0:T(8,128)S(1)} %multiply_add_fusion), kind=kOutput, calls=%fused_computation.21 | convolution fusion | flops 1610612736 | bytes 3407872 | tf_op jit(solution)/shard_map/dot_general | solution.py:31
  110.9 0.0 copy-done
  110.9 0.0 copy-start.2
  110.9 1.3 fusion.11
  112.2 0.0 copy-done.2
  112.2 0.2 fusion.18
  112.4 0.1 copy.45
  112.5 0.1 copy.47
  112.5 0.1 copy.46
  112.6 0.1 copy.44
  112.6 1.3 fusion.20
  113.9 0.0 copy-start.1
  113.9 1.3 fusion.21
  115.2 0.0 copy-done.1
  115.2 1.3 %fusion.4 = f32[1,2048,256]{2,1,0:T(8,128)S(1)} fusion(f32[2048,256]{1,0:T(8,128)S(1)} %fusion.10, bf16[256,2048]{1,0:T(8,128)(2,1)S(1)} %copy-done.1, f32[2,512,256]{2,1,0:T(8,128)S(1)} %multiply_add_fusion), kind=kOutput, calls=%fused_computation.7 | convolution fusion | flops 1611137024 | bytes 5505024 | tf_op jit(solution)/shard_map/dot_general | solution.py:31
  116.5 1.3 %fusion.5 = f32[1,2048,256]{2,1,0:T(8,128)S(1)} fusion(f32[2048,256]{1,0:T(8,128)S(1)} %fusion.11, bf16[256,2048]{1,0:T(8,128)(2,1)S(1)} %copy-done.1, f32[2,512,256]{2,1,0:T(8,128)S(1)} %multiply_add_fusion), kind=kOutput, calls=%fused_computation.9 | convolution fusion | flops 1611137024 | bytes 5505024 | tf_op jit(solution)/shard_map/dot_general | solution.py:31
  117.8 1.3 %fusion.7 = f32[1,2048,256]{2,1,0:T(8,128)S(1)} fusion(f32[2048,256]{1,0:T(8,128)S(1)} %fusion.20, bf16[256,2048]{1,0:T(8,128)(2,1)S(1)} %copy-done.1, f32[256,256]{1,0:T(8,128)S(1)} %bitcast.92), kind=kOutput, calls=%fused_computation.13 | convolution fusion | flops 1611137024 | bytes 5505024 | tf_op jit(solution)/shard_map/dot_general | solution.py:31
  119.2 0.0 copy-start.7
  119.2 0.0 copy-start.8
  119.2 1.3 %fusion.6 = f32[1,2048,256]{2,1,0:T(8,128)S(1)} fusion(f32[2048,256]{1,0:T(8,128)S(1)} %fusion.21, bf16[256,2048]{1,0:T(8,128)(2,1)S(1)} %copy-done.1, f32[256,256]{1,0:T(8,128)S(1)} %bitcast.91), kind=kOutput, calls=%fused_computation.11 | convolution fusion | flops 1611137024 | bytes 5505024 | tf_op jit(solution)/shard_map/dot_general | solution.py:31
  120.5 0.2 copy-done.7
  120.8 0.6 copy-done.8
  121.4 2.5 %fusion.8 = (bf16[2,2048,1,256]{3,1,2,0:T(8,128)(2,1)}, bf16[2,2048,1,256]{3,1,2,0:T(8,128)(2,1)}) fusion(f32[1,2048,256]{2,1,0:T(8,128)S(1)} %fusion.4, f32[1,2048,256]{2,1,0:T(8,128)S(1)} %fusion.5, bf16[2,2048,1,256]{3,1,2,0:T(8,128)(2,1)S(1)} %copy-done.7, f32[1,2048,256]{2,1,0:T(8,128)S(1)} %fusion.6, f32[1,2048,256]{2,1,0:T(8,128)S(1)} %fusion.7, ...), kind=kLoop, calls=%fused_computation.14 | loop fusion | flops 8388608 | bytes 16777216
  (1 shorter events, 0.0 us)
Async XLA Ops:
  14.3 33.0 %all-to-all-start = ((f32[8,1,32768]{2,1,0:T(1,128)}), f32[8,1,32768]{2,1,0:T(1,128)S(1)}, u32[]{:S(2)}, u32[]{:S(2)}) async-start(f32[8,1,32768]{2,1,0:T(1,128)} %reshape.42), calls=%async_computation | async-start | bytes 2097152 | tf_op jit(solution)/shard_map/all_to_all | solution.py:62
  25.7 26.2 %copy-start.9 = (s32[2]{0:T(128)S(1)}, s32[2]{0:T(128)}, u32[]{:S(2)}) copy-start(s32[2]{0:T(128)} %param.12) | copy-start | bytes 28
  28.7 25.0 %copy-start.6 = (bf16[1,512,2048]{2,1,0:T(8,128)(2,1)S(1)}, bf16[1,512,2048]{2,1,0:T(8,128)(2,1)}, u32[]{:S(2)}) copy-start(bf16[1,512,2048]{2,1,0:T(8,128)(2,1)} %param.11) | copy-start | bytes 6291460
  47.3 7.9 %copy-start.4 = (f32[8,1,32768]{2,1,0:T(1,128)}, f32[8,1,32768]{2,1,0:T(1,128)S(1)}, u32[]{:S(2)}) copy-start(f32[8,1,32768]{2,1,0:T(1,128)S(1)} %all-to-all-done) | copy-start | bytes 3145732
  47.3 29.9 %all-to-all-start.1 = ((f32[8,1,32768]{2,1,0:T(1,128)}), f32[8,1,32768]{2,1,0:T(1,128)}, u32[]{:S(2)}, u32[]{:S(2)}) async-start(f32[8,1,32768]{2,1,0:T(1,128)} %reshape.44), calls=%async_computation.1 | async-start | bytes 2097152 | tf_op jit(solution)/shard_map/all_to_all | solution.py:63
  51.6 56.8 %all-reduce.3.cloned.1.call-start = ((), (), s32[]{:S(2)}) async-start(), calls=%async_computation.2 | async-start | bytes 4194304 | tf_op jit(solution)/shard_map/psum | solution.py:13
  55.2 0.7 copy-start.10
  55.2 1.2 copy-start.5
  83.1 2.1 %copy-start.3 = (f32[2,64,1,8,256]{4,1,3,0,2:T(8,128)S(1)}, f32[2,64,1,8,256]{4,1,3,0,2:T(8,128)}, u32[]{:S(2)}) copy-start(f32[2,64,1,8,256]{4,1,3,0,2:T(8,128)} %copy.56) | copy-start | bytes 3145732
  108.4 2.6 %copy-start = (bf16[256,2048]{1,0:T(8,128)(2,1)S(1)}, bf16[256,2048]{1,0:T(8,128)(2,1)}, u32[]{:S(2)}) copy-start(bf16[256,2048]{1,0:T(8,128)(2,1)} %get-tuple-element.12) | copy-start | bytes 3145732
  110.9 1.3 copy-start.2
  113.9 1.3 copy-start.1
  119.2 1.6 %copy-start.7 = (bf16[2,2048,1,256]{3,1,2,0:T(8,128)(2,1)S(1)}, bf16[2,2048,1,256]{3,1,2,0:T(8,128)(2,1)}, u32[]{:S(2)}) copy-start(bf16[2,2048,1,256]{3,1,2,0:T(8,128)(2,1)} %param.10) | copy-start | bytes 6291460
  119.2 2.2 %copy-start.8 = (bf16[2,2048,1,256]{3,1,2,0:T(8,128)(2,1)S(1)}, bf16[2,2048,1,256]{3,1,2,0:T(8,128)(2,1)}, u32[]{:S(2)}) copy-start(bf16[2,2048,1,256]{3,1,2,0:T(8,128)(2,1)} %param.9) | copy-start | bytes 6291460
Sparse Core Ops, SparseCore 0:
  55.4 52.8 all-reduce.2
where the time goes:
time: 131 us
  waiting for transfers between devices  52.8 us (40%)
  local copies, waits for them, and re-layouts  26.2 us (20%)
  between operations  15.6 us (12%)
  other arithmetic  12.8 us (10%)
  starting transfers between devices  11.8 us (9%)
  matrix products  11.6 us (9%)
    psum x1, waiting for transfers between devices, from_root(): return lax.psum(kept, axis)  21.8 us
    unnamed x28, local copies, waits for them, and re-layouts  18.8 us
    all_to_all x1, waiting for transfers between devices, per_device(): lax.all_to_all(outgoing[0], 'pw', split_axis=3, concat_axis=1, tiled=True)  18.6 us
    all_to_all x1, waiting for transfers between devices, per_device(): lax.all_to_all(outgoing[1], 'pw', split_axis=3, concat_axis=1, tiled=True)  12.4 us
    dot_general x8, matrix products, rotate_plane(): lax.dot_general(panels[subspace_slab], block, (((0,), (0,)), ((), ())), p...  11.6 us
    all_to_all x1, starting transfers between devices, per_device(): lax.all_to_all(outgoing[0], 'pw', split_axis=3, concat_axis=1, tiled=True)  7.28 us
    all_to_all x1, other arithmetic, per_device(): lax.all_to_all(outgoing[1], 'pw', split_axis=3, concat_axis=1, tiled=True)  4.36 us
    all_to_all x1, starting transfers between devices, per_device(): lax.all_to_all(outgoing[1], 'pw', split_axis=3, concat_axis=1, tiled=True)  4.25 us
  transfers between devices with their start and end apart: 3, of which 3 were waited for; matrix products, arithmetic and copies ran while one was open for 21% of the time, Pallas kernels for 0%

commit v1 on v0

v1 whole, which is shorter than its diff:
```python
import functools

import jax
import jax.numpy as jnp
from jax import lax
from jax.experimental import pallas as pl
from jax.experimental.pallas import tpu as pltpu
from jax.sharding import PartitionSpec as P

GRID = 64
LANES = 128
PARTS = 4
TOP = 32766.0
TILE = 256
MESH = pl.DeviceIdType.MESH


def exchange_kernel(
    n, rows, chunks, keepers_ref, res_ref, loc_ref, store_ref,
    codes_ref, scales_ref, vmat_ref,
    out_codes, out_scales, masked, chip_sum, far_sum,
    code_send, code_recv, scale_send, scale_recv, own_sem,
    sib_send, sib_recv, far_send, far_recv, back_send, back_recv,
):
    me = lax.axis_index("pw")
    band = lax.axis_index("band")
    core = band % 2
    side = band // 2
    sibling = side * 2 + (1 - core)
    across = (1 - side) * 2 + core
    per_dest = chunks // n
    half = store_ref.shape[0] // 2
    part = half // PARTS
    own_start = pl.multiple_of(core * half, half)
    other_start = pl.multiple_of((1 - core) * half, half)

    barrier = pltpu.get_barrier_semaphore()

    def greet(k, _):
        d = (me + 1 + k) % n
        pl.semaphore_signal(barrier, inc=1, device_id={"pw": d}, device_id_type=MESH)
        return 0

    lax.fori_loop(0, n - 1, greet, 0)
    for peer in (sibling, across):
        pl.semaphore_signal(barrier, inc=1, device_id={"band": peer}, device_id_type=MESH)

    for panel in range(2):
        keep = (keepers_ref[panel] == band).astype(jnp.float32).astype(jnp.bfloat16)
        at = pl.ds(panel * half, half)
        masked[at, :] = store_ref[at, :] * keep
    out_scales[...] = jnp.zeros_like(out_scales)

    pl.semaphore_wait(barrier, n + 1)

    def sib_copy(q):
        return pltpu.make_async_remote_copy(
            src_ref=masked.at[pl.ds(other_start + q * part, part)],
            dst_ref=chip_sum.at[pl.ds(q * part, part)],
            send_sem=sib_send.at[q], recv_sem=sib_recv.at[q],
            device_id={"band": sibling}, device_id_type=MESH,
        )

    def far_copy(q):
        return pltpu.make_async_remote_copy(
            src_ref=masked.at[pl.ds(own_start + q * part, part)],
            dst_ref=far_sum.at[pl.ds(q * part, part)],
            send_sem=far_send.at[q], recv_sem=far_recv.at[q],
            device_id={"band": across}, device_id_type=MESH,
        )

    def back_copy(q):
        at = pl.ds(own_start + q * part, part)
        return pltpu.make_async_remote_copy(
            src_ref=vmat_ref.at[at], dst_ref=vmat_ref.at[at],
            send_sem=back_send.at[q], recv_sem=back_recv.at[q],
            device_id={"band": sibling}, device_id_type=MESH,
        )

    def back_arrival(q):
        at = pl.ds(other_start + q * part, part)
        return pltpu.make_async_remote_copy(
            src_ref=vmat_ref.at[at], dst_ref=vmat_ref.at[at],
            send_sem=back_send.at[q], recv_sem=back_recv.at[q],
            device_id={"band": sibling}, device_id_type=MESH,
        )

    for q in range(PARTS):
        sib_copy(q).start()

    def code_copy(k, d):
        return pltpu.make_async_remote_copy(
            src_ref=out_codes.at[d], dst_ref=codes_ref.at[me],
            send_sem=code_send.at[k], recv_sem=code_recv.at[k],
            device_id={"pw": d}, device_id_type=MESH,
        )

    def scale_copy(k, d):
        return pltpu.make_async_remote_copy(
            src_ref=out_scales.at[d], dst_ref=scales_ref.at[me],
            send_sem=scale_send.at[k], recv_sem=scale_recv.at[k],
            device_id={"pw": d}, device_id_type=MESH,
        )

    own_codes = pltpu.make_async_copy(out_codes.at[me], codes_ref.at[me], own_sem.at[0])
    own_scales = pltpu.make_async_copy(out_scales.at[me], scales_ref.at[me], own_sem.at[1])

    def send(k, _):
        d = (me + n // 2 + k) % n
        for a, ref in enumerate((res_ref, loc_ref)):
            for c in range(per_dest):
                lane = pl.ds(c * LANES, LANES)
                both = []
                for plane in range(2):
                    first = plane * rows * chunks + d * per_dest + c
                    x = ref[pl.ds(first, rows, stride=chunks), :]
                    top = jnp.max(jnp.abs(x), axis=0, keepdims=True)
                    inv = jnp.where(top > 1e-30, TOP / jnp.maximum(top, 1e-30), 0.0)
                    both.append(jnp.floor(x * inv + 0.5).astype(jnp.int32))
                    out_scales[d, pl.ds(a * 2 + plane, 1), lane] = top * (1.0 / TOP)
                q = jnp.concatenate(both, axis=0).astype(jnp.int16)
                out_codes[d, pl.ds(a * 2 * rows, 2 * rows), lane] = q

        @pl.when(k != n // 2)
        def _():
            scale_copy(k, d).start()
            code_copy(k, d).start()

        @pl.when(k == n // 2)
        def _():
            own_scales.start()
            own_codes.start()

        return 0

    lax.fori_loop(0, n // 2, send, 0)
    for q in range(PARTS):
        sib_copy(q).wait_recv()
        mine = pl.ds(own_start + q * part, part)
        masked[mine, :] = masked[mine, :] + chip_sum[pl.ds(q * part, part), :]
        far_copy(q).start()
    lax.fori_loop(n // 2, n, send, 0)

    for q in range(PARTS):
        far_copy(q).wait_recv()
        mine = pl.ds(own_start + q * part, part)
        vmat_ref[mine, :] = masked[mine, :] + far_sum[pl.ds(q * part, part), :]
        back_copy(q).start()

    def finish(k, _):
        d = (me + n // 2 + k) % n

        @pl.when(k != n // 2)
        def _():
            scale_copy(k, d).wait()
            code_copy(k, d).wait()

        return 0

    lax.fori_loop(0, n, finish, 0)
    own_scales.wait()
    own_codes.wait()
    for q in range(PARTS):
        sib_copy(q).wait_send()
        far_copy(q).wait_send()
        back_copy(q).wait_send()
        back_arrival(q).wait_recv()


def exchange(n, keepers, res, loc, store):
    planes, rows, _, width = res.shape
    chunks = width // LANES
    span = store.shape[2]
    depth = store.shape[1]
    blocks = 2 * planes * rows
    cols = width // n
    flat = (planes * rows * chunks, LANES)
    dma = pltpu.SemaphoreType.DMA
    vmem = pl.BlockSpec(memory_space=pltpu.VMEM)
    return pl.pallas_call(
        functools.partial(exchange_kernel, n, rows, chunks),
        out_shape=(
            jax.ShapeDtypeStruct((n, blocks, cols), jnp.int16),
            jax.ShapeDtypeStruct((n, 8, cols), jnp.float32),
            jax.ShapeDtypeStruct((depth, span), jnp.bfloat16),
        ),
        in_specs=[pl.BlockSpec(memory_space=pltpu.SMEM), vmem, vmem, vmem],
        out_specs=(
            pl.BlockSpec(memory_space=pl.ANY),
            pl.BlockSpec(memory_space=pl.ANY),
            vmem,
        ),
        scratch_shapes=[
            pltpu.VMEM((n, blocks, cols), jnp.int16),
            pltpu.VMEM((n, 8, cols), jnp.float32),
            pltpu.VMEM((depth, span), jnp.bfloat16),
            pltpu.VMEM((depth // 2, span), jnp.bfloat16),
            pltpu.VMEM((depth // 2, span), jnp.bfloat16),
            dma((n,)), dma((n,)), dma((n,)), dma((n,)), dma((2,)),
            dma((PARTS,)), dma((PARTS,)), dma((PARTS,)), dma((PARTS,)),
            dma((PARTS,)), dma((PARTS,)),
        ],
        compiler_params=pltpu.CompilerParams(
            collective_id=0, has_side_effects=True, vmem_limit_bytes=40 * 2**20
        ),
    )(keepers, res.reshape(flat), loc.reshape(flat), store.reshape(depth, span))


def kinetic_of(lattice_position):
    first = lattice_position // (GRID * GRID)
    second = lattice_position // GRID % GRID
    third = lattice_position % GRID
    total = jnp.zeros(lattice_position.shape, jnp.int32)
    for index in (first, second, third):
        folded = jnp.where(index >= GRID // 2, index - GRID, index)
        total = total + folded * folded
    return total.astype(jnp.float32) / (GRID * GRID)


def rotate_kernel(
    n, rows, codes_ref, scales_ref, kinetic_ref, vmat_ref, psi_ref, hpsi_ref,
    psi_out, hpsi_out, high, low,
):
    cols = codes_ref.shape[2]
    group = max(1, 16 // rows)

    @pl.when(pl.program_id(0) == 0)
    def _():
        kinetic = kinetic_ref[...]

        def columns(s):
            codes = codes_ref[s].astype(jnp.int32).astype(jnp.float32)
            scales = scales_ref[s]
            values = [
                codes[b * rows : (b + 1) * rows] * scales[b : b + 1] for b in range(4)
            ]
            for plane in range(2):
                values[2 + plane] = kinetic * values[plane] + values[2 + plane]
            return jnp.concatenate(values, axis=1)

        def unpack(step, _):
            both = jnp.concatenate(
                [columns(step * group + i) for i in range(group)], axis=0
            )
            top = both.astype(jnp.bfloat16)
            at = pl.ds(pl.multiple_of(step * group * rows, group * rows), group * rows)
            high[at, :] = top
            low[at, :] = (both - top.astype(jnp.float32)).astype(jnp.bfloat16)
            return 0

        lax.fori_loop(0, n // group, unpack, 0)

    dims = (((0,), (0,)), ((), ()))
    v = vmat_ref[...]
    total = lax.dot_general(v, high[...], dims, preferred_element_type=jnp.float32)
    total = total + lax.dot_general(v, low[...], dims, preferred_element_type=jnp.float32)
    for plane in range(2):
        psi = total[:, plane * cols : (plane + 1) * cols]
        hpsi = total[:, (2 + plane) * cols : (3 + plane) * cols]
        psi_out[plane] = (psi_ref[plane].astype(jnp.float32) + psi).astype(jnp.bfloat16)
        hpsi_out[plane] = (hpsi_ref[plane].astype(jnp.float32) + hpsi).astype(jnp.bfloat16)


def rotate(codes, scales, kinetic, vmat, psi, hpsi):
    n, blocks, cols = codes.shape
    rows = blocks // 4
    depth, span = vmat.shape
    whole = lambda shape: pl.BlockSpec(shape, lambda j: (0,) * len(shape))
    band_tile = pl.BlockSpec((2, TILE, cols), lambda j: (0, j, 0))
    out = jax.ShapeDtypeStruct((2, span, cols), jnp.bfloat16)
    return pl.pallas_call(
        functools.partial(rotate_kernel, n, rows),
        grid=(span // TILE,),
        out_shape=(out, out),
        in_specs=[
            whole((n, blocks, cols)),
            whole((n, 8, cols)),
            whole((1, cols)),
            pl.BlockSpec((depth, TILE), lambda j: (0, j)),
            band_tile,
            band_tile,
        ],
        out_specs=(band_tile, band_tile),
        scratch_shapes=[
            pltpu.VMEM((depth, 4 * cols), jnp.bfloat16),
            pltpu.VMEM((depth, 4 * cols), jnp.bfloat16),
        ],
        compiler_params=pltpu.CompilerParams(vmem_limit_bytes=40 * 2**20),
    )(codes, scales, kinetic, vmat, psi, hpsi)


def per_device(n, res, loc, psi, hpsi, store, keepers, lattice):
    codes, scales, vmat = exchange(n, keepers, res, loc, store)
    planes, span, _, cols = psi.shape
    kinetic = kinetic_of(lattice)
    flat = (planes, span, cols)
    psi_new, hpsi_new = rotate(
        codes, scales, kinetic, vmat, psi.reshape(flat), hpsi.reshape(flat)
    )
    return psi_new.reshape(psi.shape), hpsi_new.reshape(hpsi.shape)


def solution(mesh):
    in_specs = (
        P(None, "pw", "band", None),
        P(None, "pw", "band", None),
        P(None, None, "band", "pw"),
        P(None, None, "band", "pw"),
        P("band", None, None),
        P(),
        P("band", "pw"),
    )
    out_specs = (P(None, None, "band", "pw"), P(None, None, "band", "pw"))
    return jax.shard_map(
        functools.partial(per_device, mesh.shape["pw"]),
        mesh=mesh, in_specs=in_specs, out_specs=out_specs, check_vma=False,
    )
```

time: 131 us -> 48.5 us (0.37)
  waiting for transfers between devices: 52.8 us -> 0 us
  Pallas kernels: 0 us -> 42.2 us
  local copies, waits for them, and re-layouts: 26.2 us -> 4.7 us
  between operations: 15.6 us -> 0.67 us
  other arithmetic: 12.8 us -> 0.71 us
  starting transfers between devices: 11.8 us -> 0 us
  matrix products: 11.6 us -> 0 us
    pallas_call x0 -> x2, Pallas kernels: none -> 42.2 us  [the longest x1 34.1 us: exchange(): pl.pallas_call(functools.partial(exchange_kernel, n, rows, chunks), out_s...]
    all_to_all x2 -> x0, waiting for transfers between devices: 31 us -> none  [the longest x1 18.6 us: per_device(): lax.all_to_all(outgoing[0], 'pw', split_axis=3, concat_axis=1, tiled=True)]
    psum x1 -> x0, waiting for transfers between devices: 21.8 us -> none  [from_root(): return lax.psum(kept, axis)]
    unnamed x28 -> x12, local copies, waits for them, and re-layouts: 18.8 us -> 4.7 us
    dot_general x8 -> x0, matrix products: 11.6 us -> none  [rotate_plane(): lax.dot_general(panels[subspace_slab], block, (((0,), (0,)), ((), ())), p...]
    all_to_all x2 -> x0, starting transfers between devices: 11.5 us -> none  [the longest x1 7.28 us: per_device(): lax.all_to_all(outgoing[0], 'pw', split_axis=3, concat_axis=1, tiled=True)]
    all_to_all x2 -> x0, other arithmetic: 7.48 us -> none  [the longest x1 4.36 us: per_device(): lax.all_to_all(outgoing[1], 'pw', split_axis=3, concat_axis=1, tiled=True)]
    all_to_all x4 -> x0, local copies, waits for them, and re-layouts: 6.38 us -> none  [the longest x2 3.75 us: per_device(): lax.all_to_all(outgoing[0], 'pw', split_axis=3, concat_axis=1, tiled=True)]
  transfers between devices with their start and end apart: 3 -> 0, of which waited for: 3 -> 0; matrix products, arithmetic and copies ran while one was open for 21% -> 0% of each run, Pallas kernels for 0% -> 0%
where the time goes in v1:
time: 48.5 us; the launch traced here: 48.2 us
  Pallas kernels  42.2 us (87%)
  local copies, waits for them, and re-layouts  4.7 us (10%)
  other arithmetic  0.71 us (1%)
  between operations  0.67 us (1%)
    pallas_call x1, Pallas kernels, exchange(): pl.pallas_call(functools.partial(exchange_kernel, n, rows, chunks), out_s...  34.1 us
    pallas_call x1, Pallas kernels, rotate(): pl.pallas_call(functools.partial(rotate_kernel, n, rows), grid=(span // T...  8.03 us
    unnamed x12, local copies, waits for them, and re-layouts  4.7 us

profile of v1, /device:TPU:0, one launch (start us, length us, event | category | flops | bytes accessed | tf_op | source)
XLA Modules:
  0.0 48.2 jit_solution(4991303977666951135)
XLA Ops:
  0.6 0.7 %convert_multiply_fusion.kinetic_ref = f32[1,256]{1,0:T(1,128)S(1)} fusion(s32[1,256]{1,0:T(1,128)} %param.13), kind=kLoop, calls=%fused_computation.20 | loop fusion | flops 14336 | bytes 2048 | tf_op jit(solution)/shard_map/div | solution.py:217
  1.3 0.0 copy-start
  1.3 1.6 %copy-done = bf16[1,512,2048]{2,1,0:T(8,128)(2,1)S(1)} copy-done((bf16[1,512,2048]{2,1,0:T(8,128)(2,1)S(1)}, bf16[1,512,2048]{2,1,0:T(8,128)(2,1)}, u32[]{:S(2)}) %copy-start) | copy-done | bytes 2097176
  2.9 0.0 copy-start.3
  2.9 1.2 %copy-done.3 = f32[2,64,1,2048]{3,2,1,0:T(1,128)S(1)} copy-done((f32[2,64,1,2048]{3,2,1,0:T(1,128)S(1)}, f32[2,64,1,2048]{3,2,1,0:T(1,128)}, u32[]{:S(2)}) %copy-start.3) | copy-done | bytes 1048600
  4.2 0.0 copy-start.4
  4.2 1.2 %copy-done.4 = f32[2,64,1,2048]{3,2,1,0:T(1,128)S(1)} copy-done((f32[2,64,1,2048]{3,2,1,0:T(1,128)S(1)}, f32[2,64,1,2048]{3,2,1,0:T(1,128)}, u32[]{:S(2)}) %copy-start.4) | copy-done | bytes 1048600
  5.4 0.0 copy-start.5
  5.4 0.7 %copy-done.5 = s32[2]{0:T(128)S(1)} copy-done((s32[2]{0:T(128)S(1)}, s32[2]{0:T(128)}, u32[]{:S(2)}) %copy-start.5) | copy-done | bytes 32
  6.0 0.0 copy-start.1
  6.0 0.0 copy-start.2
  6.0 34.1 %shard_map.86 = (s16[8,256,256]{2,1,0:T(8,128)(2,1)S(1)}, f32[8,8,256]{2,1,0:T(8,128)S(1)}, bf16[512,2048]{1,0:T(8,128)(2,1)S(1)}) custom-call(s32[2]{0:T(128)S(1)} %copy-done.5, f32[2048,128]{1,0:T(8,128)S(1)} %bitcast.14, f32[2048,128]{1,0:T(8,128)S(1)} %bitcast.15, bf16[512,2048]{1,0:T(8,128)(2,1)S(1)} %bitcast.11), custom_call_target="tpu_custom_call" | custom-call | tf_op jit(solution)/shard_map/pallas_call | solution.py:180
  40.2 0.0 copy-done.1
  40.2 0.0 copy-done.2
  40.2 8.0 %shard_map.87 = (bf16[2,2048,256]{2,1,0:T(8,128)(2,1)}, bf16[2,2048,256]{2,1,0:T(8,128)(2,1)}) custom-call(s16[8,256,256]{2,1,0:T(8,128)(2,1)S(1)} %get-tuple-element.7.codes_ref, f32[8,8,256]{2,1,0:T(8,128)S(1)} %get-tuple-element.8.scales_ref, f32[1,256]{1,0:T(1,128)S(1)} %convert_multiply_fusion.kinetic_ref, ...), custom_call_target="tpu_custom_call" | custom-call | tf_op jit(solution)/shard_map/pallas_call | solution.py:271
Async XLA Ops:
  1.3 1.6 %copy-start = (bf16[1,512,2048]{2,1,0:T(8,128)(2,1)S(1)}, bf16[1,512,2048]{2,1,0:T(8,128)(2,1)}, u32[]{:S(2)}) copy-start(bf16[1,512,2048]{2,1,0:T(8,128)(2,1)} %param.11) | copy-start | bytes 6291460
  2.9 1.2 %copy-start.3 = (f32[2,64,1,2048]{3,2,1,0:T(1,128)S(1)}, f32[2,64,1,2048]{3,2,1,0:T(1,128)}, u32[]{:S(2)}) copy-start(f32[2,64,1,2048]{3,2,1,0:T(1,128)} %param.7) | copy-start | bytes 3145732
  4.2 1.2 %copy-start.4 = (f32[2,64,1,2048]{3,2,1,0:T(1,128)S(1)}, f32[2,64,1,2048]{3,2,1,0:T(1,128)}, u32[]{:S(2)}) copy-start(f32[2,64,1,2048]{3,2,1,0:T(1,128)} %param.8) | copy-start | bytes 3145732
  5.4 0.7 %copy-start.5 = (s32[2]{0:T(128)S(1)}, s32[2]{0:T(128)}, u32[]{:S(2)}) copy-start(s32[2]{0:T(128)} %keepers_ref.1) | copy-start | bytes 28
  6.0 34.2 %copy-start.1 = (bf16[2,2048,1,256]{3,1,2,0:T(8,128)(2,1)S(1)}, bf16[2,2048,1,256]{3,1,2,0:T(8,128)(2,1)}, u32[]{:S(2)}) copy-start(bf16[2,2048,1,256]{3,1,2,0:T(8,128)(2,1)} %param.9) | copy-start | bytes 6291460
  6.0 34.2 %copy-start.2 = (bf16[2,2048,1,256]{3,1,2,0:T(8,128)(2,1)S(1)}, bf16[2,2048,1,256]{3,1,2,0:T(8,128)(2,1)}, u32[]{:S(2)}) copy-start(bf16[2,2048,1,256]{3,1,2,0:T(8,128)(2,1)} %param.10) | copy-start | bytes 6291460

commit v2 on v0

v2 whole, which is shorter than its diff:
```python
import functools

import jax
import jax.numpy as jnp
from jax import lax
from jax.experimental import pallas as pl
from jax.experimental.pallas import tpu as pltpu
from jax.sharding import PartitionSpec as P

GRID = 64
LANES = 128
PARTS = 4
TOP = 32766.0
TILE = 256
MESH = pl.DeviceIdType.MESH


def kinetic_of(lattice_position):
    first = lattice_position // (GRID * GRID)
    second = lattice_position // GRID % GRID
    third = lattice_position % GRID
    total = jnp.zeros(lattice_position.shape, jnp.int32)
    for index in (first, second, third):
        folded = jnp.where(index >= GRID // 2, index - GRID, index)
        total = total + folded * folded
    return total.astype(jnp.float32) / (GRID * GRID)


def rotated(v, high, low):
    dims = (((0,), (0,)), ((), ()))
    total = lax.dot_general(v, high, dims, preferred_element_type=jnp.float32)
    return total + lax.dot_general(v, low, dims, preferred_element_type=jnp.float32)


def exchange_kernel(
    n, rows, chunks,
    keepers_hbm, res_hbm, loc_hbm, store_hbm, kinetic_ref, psi_hbm, hpsi_hbm,
    vmat_ref, high1_ref, low1_ref, psi0_ref, hpsi0_ref,
    keepers, res, loc, masked, psi_sum, hpsi_sum,
    out_codes, out_scales, codes, scales, chip_sum, far_sum, high0, low0,
    load_sem, code_send, code_recv, scale_send, scale_recv,
    sib_send, sib_recv, far_send, far_recv, side_send, side_recv, back_send, back_recv,
):
    me = lax.axis_index("pw")
    band = lax.axis_index("band")
    core = band % 2
    side = band // 2
    sibling = side * 2 + (1 - core)
    across = (1 - side) * 2 + core
    parity = me % 2
    beside = me + 1 - 2 * parity
    per_dest = chunks // n
    cols = per_dest * LANES
    half = masked.shape[0] // 2
    part = half // PARTS
    own_start = pl.multiple_of(core * half, half)
    other_start = pl.multiple_of((1 - core) * half, half)

    loads = [
        pltpu.make_async_copy(src, dst, load_sem.at[i])
        for i, (src, dst) in enumerate(
            (
                (keepers_hbm, keepers),
                (res_hbm, res),
                (loc_hbm, loc),
                (store_hbm, masked),
                (psi_hbm.at[0], psi_sum),
                (hpsi_hbm.at[0], hpsi_sum),
            )
        )
    ]
    for load in loads[:4]:
        load.start()

    barrier = pltpu.get_barrier_semaphore()

    def greet(k, _):
        d = (me + 1 + k) % n
        pl.semaphore_signal(barrier, inc=1, device_id={"pw": d}, device_id_type=MESH)
        return 0

    lax.fori_loop(0, n - 1, greet, 0)
    for peer in (sibling, across):
        pl.semaphore_signal(barrier, inc=1, device_id={"band": peer}, device_id_type=MESH)
    out_scales[...] = jnp.zeros_like(out_scales)

    def sib_copy(q):
        return pltpu.make_async_remote_copy(
            src_ref=masked.at[pl.ds(other_start + q * part, part)],
            dst_ref=chip_sum.at[pl.ds(q * part, part)],
            send_sem=sib_send.at[q], recv_sem=sib_recv.at[q],
            device_id={"band": sibling}, device_id_type=MESH,
        )

    def far_copy(i, q):
        return pltpu.make_async_remote_copy(
            src_ref=masked.at[pl.ds(own_start + q * part, part)],
            dst_ref=far_sum.at[pl.ds(q * part, part)],
            send_sem=far_send.at[i], recv_sem=far_recv.at[i],
            device_id={"band": across}, device_id_type=MESH,
        )

    def side_copy(q):
        at = pl.ds(own_start + q * part, part)
        return pltpu.make_async_remote_copy(
            src_ref=vmat_ref.at[at], dst_ref=vmat_ref.at[at],
            send_sem=side_send, recv_sem=side_recv,
            device_id={"pw": beside}, device_id_type=MESH,
        )

    def back_copy(i, start, q):
        at = pl.ds(start + q * part, part)
        return pltpu.make_async_remote_copy(
            src_ref=vmat_ref.at[at], dst_ref=vmat_ref.at[at],
            send_sem=back_send.at[i], recv_sem=back_recv.at[i],
            device_id={"band": sibling}, device_id_type=MESH,
        )

    fetched = (2 + parity, 0, 1, 3 - parity)

    def code_copy(plane, k, d):
        return pltpu.make_async_remote_copy(
            src_ref=out_codes.at[plane, d], dst_ref=codes.at[plane, me],
            send_sem=code_send.at[plane, k], recv_sem=code_recv.at[plane, k],
            device_id={"pw": d}, device_id_type=MESH,
        )

    def scale_copy(plane, k, d):
        return pltpu.make_async_remote_copy(
            src_ref=out_scales.at[plane, d], dst_ref=scales.at[plane, me],
            send_sem=scale_send.at[plane, k], recv_sem=scale_recv.at[plane, k],
            device_id={"pw": d}, device_id_type=MESH,
        )

    def send(plane, k, _):
        d = (me + n // 2 + k) % n
        for c in range(per_dest):
            lane = pl.ds(c * LANES, LANES)
            both, tops = [], []
            for ref in (res, loc):
                first = plane * rows * chunks + d * per_dest + c
                x = ref[pl.ds(first, rows, stride=chunks), :]
                top = jnp.max(jnp.abs(x), axis=0, keepdims=True)
                inv = jnp.where(top > 1e-30, TOP / jnp.maximum(top, 1e-30), 0.0)
                both.append(jnp.floor(x * inv + 0.5).astype(jnp.int32))
                tops.append(top * (1.0 / TOP))
            q = jnp.concatenate(both, axis=0).astype(jnp.int16)

            @pl.when(k != n // 2)
            def _():
                out_codes[plane, d, :, lane] = q
                for a in range(2):
                    out_scales[plane, d, pl.ds(a, 1), lane] = tops[a]

            @pl.when(k == n // 2)
            def _():
                codes[plane, me, :, lane] = q
                for a in range(2):
                    scales[plane, me, pl.ds(a, 1), lane] = tops[a]

        @pl.when(k != n // 2)
        def _():
            scale_copy(plane, k, d).start()
            code_copy(plane, k, d).start()

        return 0

    def arrive(plane, k, _):
        d = (me + n // 2 + k) % n

        @pl.when(k != n // 2)
        def _():
            scale_copy(plane, k, d).wait()
            code_copy(plane, k, d).wait()

        return 0

    def unpack(plane, high, low):
        kinetic = kinetic_of(kinetic_ref[...])
        group = max(1, 16 // rows)

        def columns(s):
            q = codes[plane, s].astype(jnp.int32).astype(jnp.float32)
            scale = scales[plane, s]
            corr = q[:rows] * scale[0:1]
            other = q[rows:] * scale[1:2]
            return jnp.concatenate([corr, kinetic * corr + other], axis=1)

        def step(i, _):
            both = jnp.concatenate([columns(i * group + j) for j in range(group)], axis=0)
            top = both.astype(jnp.bfloat16)
            at = pl.ds(pl.multiple_of(i * group * rows, group * rows), group * rows)
            high[at, :] = top
            low[at, :] = (both - top.astype(jnp.float32)).astype(jnp.bfloat16)
            return 0

        lax.fori_loop(0, n // group, step, 0)

    loads[1].wait()
    loads[2].wait()
    pl.semaphore_wait(barrier, n + 1)
    lax.fori_loop(0, n // 2, functools.partial(send, 0), 0)

    loads[0].wait()
    loads[3].wait()
    for panel in range(2):
        keep = (keepers[panel] == band).astype(jnp.float32).astype(jnp.bfloat16)
        at = pl.ds(panel * half, half)
        masked[at, :] = masked[at, :] * keep
    for q in range(PARTS):
        sib_copy(q).start()
    lax.fori_loop(n // 2, n, functools.partial(send, 0), 0)
    for q in range(PARTS):
        sib_copy(q).wait()
    mine = pl.ds(own_start, half)
    masked[mine, :] = masked[mine, :] + chip_sum[...]
    for i in range(3):
        far_copy(i, fetched[i]).start()
    lax.fori_loop(0, n, functools.partial(send, 1), 0)
    for load in loads[4:]:
        load.start()

    for i in range(3):
        far_copy(i, fetched[i]).wait_recv()
        at = pl.ds(pl.multiple_of(own_start + fetched[i] * part, part), part)
        near = pl.ds(pl.multiple_of(fetched[i] * part, part), part)
        vmat_ref[at, :] = masked[at, :] + far_sum[near, :]
        if i == 0:
            side_copy(fetched[0]).start()
        back_copy(i, own_start, fetched[i]).start()
    side_copy(fetched[0]).wait_send()
    side_copy(fetched[3]).wait_recv()
    back_copy(3, own_start, fetched[3]).start()

    lax.fori_loop(0, n, functools.partial(arrive, 0), 0)
    unpack(0, high0, low0)
    for i in range(PARTS):
        back_copy(i, other_start, fetched[i]).wait_recv()
    for load in loads[4:]:
        load.wait()

    def tile(j, _):
        at = pl.ds(pl.multiple_of(j * TILE, TILE), TILE)
        total = rotated(vmat_ref[:, at], high0[...], low0[...])
        psi0_ref[at, :] = (psi_sum[at, :].astype(jnp.float32) + total[:, :cols]).astype(jnp.bfloat16)
        hpsi0_ref[at, :] = (hpsi_sum[at, :].astype(jnp.float32) + total[:, cols:]).astype(jnp.bfloat16)
        return 0

    lax.fori_loop(0, vmat_ref.shape[1] // TILE, tile, 0)

    lax.fori_loop(0, n, functools.partial(arrive, 1), 0)
    unpack(1, high1_ref, low1_ref)
    for i in range(3):
        far_copy(i, fetched[i]).wait_send()
    for i in range(PARTS):
        back_copy(i, own_start, fetched[i]).wait_send()


def exchange(n, keepers, res, loc, store, lattice, psi, hpsi):
    planes, rows, _, width = res.shape
    chunks = width // LANES
    depth, span = store.shape[1:]
    cols = width // n
    flat = (planes * rows * chunks, LANES)
    dma = pltpu.SemaphoreType.DMA
    vmem = pl.BlockSpec(memory_space=pltpu.VMEM)
    hbm = pl.BlockSpec(memory_space=pltpu.HBM)
    parts = jax.ShapeDtypeStruct((depth, 2 * cols), jnp.bfloat16)
    plane = jax.ShapeDtypeStruct((span, cols), jnp.bfloat16)
    return pl.pallas_call(
        functools.partial(exchange_kernel, n, rows, chunks),
        out_shape=(
            jax.ShapeDtypeStruct((depth, span), jnp.bfloat16), parts, parts, plane, plane,
        ),
        in_specs=[hbm, hbm, hbm, hbm, vmem, hbm, hbm],
        out_specs=(vmem,) * 5,
        scratch_shapes=[
            pltpu.SMEM((2,), jnp.int32),
            pltpu.VMEM(flat, jnp.float32),
            pltpu.VMEM(flat, jnp.float32),
            pltpu.VMEM((depth, span), jnp.bfloat16),
            pltpu.VMEM((span, cols), jnp.bfloat16),
            pltpu.VMEM((span, cols), jnp.bfloat16),
            pltpu.VMEM((planes, n, 2 * rows, cols), jnp.int16),
            pltpu.VMEM((planes, n, 8, cols), jnp.float32),
            pltpu.VMEM((planes, n, 2 * rows, cols), jnp.int16),
            pltpu.VMEM((planes, n, 8, cols), jnp.float32),
            pltpu.VMEM((depth // 2, span), jnp.bfloat16),
            pltpu.VMEM((depth // 2, span), jnp.bfloat16),
            pltpu.VMEM((depth, 2 * cols), jnp.bfloat16),
            pltpu.VMEM((depth, 2 * cols), jnp.bfloat16),
            dma((6,)), dma((planes, n)), dma((planes, n)), dma((planes, n)), dma((planes, n)),
            dma((PARTS,)), dma((PARTS,)), dma((3,)), dma((3,)), dma, dma,
            dma((PARTS,)), dma((PARTS,)),
        ],
        compiler_params=pltpu.CompilerParams(
            collective_id=0, has_side_effects=True, vmem_limit_bytes=50 * 2**20
        ),
    )(
        keepers, res.reshape(flat), loc.reshape(flat), store.reshape(depth, span),
        lattice, psi, hpsi,
    )


def rotate_kernel(
    vmat_ref, high_ref, low_ref, psi0_ref, hpsi0_ref, psi_ref, hpsi_ref, psi_out, hpsi_out
):
    cols = psi0_ref.shape[1]
    total = rotated(vmat_ref[...], high_ref[...], low_ref[...])
    psi_out[0] = psi0_ref[...]
    hpsi_out[0] = hpsi0_ref[...]
    psi_out[1] = (psi_ref[0].astype(jnp.float32) + total[:, :cols]).astype(jnp.bfloat16)
    hpsi_out[1] = (hpsi_ref[0].astype(jnp.float32) + total[:, cols:]).astype(jnp.bfloat16)


def rotate(vmat, high, low, psi0, hpsi0, psi, hpsi):
    depth, span = vmat.shape
    cols = psi0.shape[1]
    halves = pl.BlockSpec((depth, 2 * cols), lambda j: (0, 0))
    done = pl.BlockSpec((TILE, cols), lambda j: (j, 0))
    second = pl.BlockSpec((1, TILE, cols), lambda j: (1, j, 0))
    band_tile = pl.BlockSpec((2, TILE, cols), lambda j: (0, j, 0))
    out = jax.ShapeDtypeStruct((2, span, cols), jnp.bfloat16)
    return pl.pallas_call(
        rotate_kernel,
        grid=(span // TILE,),
        out_shape=(out, out),
        in_specs=[
            pl.BlockSpec((depth, TILE), lambda j: (0, j)),
            halves, halves, done, done, second, second,
        ],
        out_specs=(band_tile, band_tile),
        compiler_params=pltpu.CompilerParams(vmem_limit_bytes=40 * 2**20),
    )(vmat, high, low, psi0, hpsi0, psi, hpsi)


def per_device(n, res, loc, psi, hpsi, store, keepers, lattice):
    planes, span, _, cols = psi.shape
    psi_in, hpsi_in = (x.reshape(planes, span, cols) for x in (psi, hpsi))
    vmat, high, low, psi0, hpsi0 = exchange(
        n, keepers, res, loc, store, lattice, psi_in, hpsi_in
    )
    psi_new, hpsi_new = rotate(vmat, high, low, psi0, hpsi0, psi_in, hpsi_in)
    return psi_new.reshape(psi.shape), hpsi_new.reshape(hpsi.shape)


def solution(mesh):
    in_specs = (
        P(None, "pw", "band", None),
        P(None, "pw", "band", None),
        P(None, None, "band", "pw"),
        P(None, None, "band", "pw"),
        P("band", None, None),
        P(),
        P("band", "pw"),
    )
    out_specs = (P(None, None, "band", "pw"), P(None, None, "band", "pw"))
    return jax.shard_map(
        functools.partial(per_device, mesh.shape["pw"]),
        mesh=mesh, in_specs=in_specs, out_specs=out_specs, check_vma=False,
    )
```

time: 131 us -> 46 us (0.35)
  waiting for transfers between devices: 52.8 us -> 0 us
  Pallas kernels: 0 us -> 42 us
  local copies, waits for them, and re-layouts: 26.2 us -> 2.92 us
  between operations: 15.6 us -> 0.67 us
  other arithmetic: 12.8 us -> 0 us
  starting transfers between devices: 11.8 us -> 0 us
  matrix products: 11.6 us -> 0 us
    pallas_call x0 -> x2, Pallas kernels: none -> 42 us  [the longest x1 36.3 us: exchange(): pl.pallas_call(functools.partial(exchange_kernel, n, rows, chunks), out_s...]
    all_to_all x2 -> x0, waiting for transfers between devices: 31 us -> none  [the longest x1 18.6 us: per_device(): lax.all_to_all(outgoing[0], 'pw', split_axis=3, concat_axis=1, tiled=True)]
    psum x1 -> x0, waiting for transfers between devices: 21.8 us -> none  [from_root(): return lax.psum(kept, axis)]
    unnamed x28 -> x10, local copies, waits for them, and re-layouts: 18.8 us -> 2.92 us
    dot_general x8 -> x0, matrix products: 11.6 us -> none  [rotate_plane(): lax.dot_general(panels[subspace_slab], block, (((0,), (0,)), ((), ())), p...]
    all_to_all x2 -> x0, starting transfers between devices: 11.5 us -> none  [the longest x1 7.28 us: per_device(): lax.all_to_all(outgoing[0], 'pw', split_axis=3, concat_axis=1, tiled=True)]
    all_to_all x2 -> x0, other arithmetic: 7.48 us -> none  [the longest x1 4.36 us: per_device(): lax.all_to_all(outgoing[1], 'pw', split_axis=3, concat_axis=1, tiled=True)]
    all_to_all x4 -> x0, local copies, waits for them, and re-layouts: 6.38 us -> none  [the longest x2 3.75 us: per_device(): lax.all_to_all(outgoing[0], 'pw', split_axis=3, concat_axis=1, tiled=True)]
  transfers between devices with their start and end apart: 3 -> 0, of which waited for: 3 -> 0; matrix products, arithmetic and copies ran while one was open for 21% -> 0% of each run, Pallas kernels for 0% -> 0%
where the time goes in v2:
time: 46 us; the launch traced here: 45.6 us
  Pallas kernels  42 us (91%)
  local copies, waits for them, and re-layouts  2.92 us (6%)
  between operations  0.67 us (1%)
    pallas_call x1, Pallas kernels, exchange(): pl.pallas_call(functools.partial(exchange_kernel, n, rows, chunks), out_s...  36.3 us
    pallas_call x1, Pallas kernels, rotate(): pl.pallas_call(rotate_kernel, grid=(span // TILE,), out_shape=(out, out),...  5.68 us
    unnamed x10, local copies, waits for them, and re-layouts  2.92 us

profile of v2, /device:TPU:0, one launch (start us, length us, event | category | flops | bytes accessed | tf_op | source)
XLA Modules:
  0.0 45.6 jit_solution(14703953341936257072)
XLA Ops:
  0.6 0.0 copy-start.3
  0.6 0.7 %copy-done.3 = s32[1,256]{1,0:T(1,128)S(1)} copy-done((s32[1,256]{1,0:T(1,128)S(1)}, s32[1,256]{1,0:T(1,128)}, u32[]{:S(2)}) %copy-start.3) | copy-done | bytes 1048
  1.3 0.0 copy-start.4
  1.3 0.7 %copy-done.4 = s32[2]{0:T(128)S(1)} copy-done((s32[2]{0:T(128)S(1)}, s32[2]{0:T(128)}, u32[]{:S(2)}) %copy-start.4) | copy-done | bytes 32
  2.0 0.0 copy-start
  2.0 0.0 copy-start.1
  2.0 36.3 %shard_map.86 = (bf16[512,2048]{1,0:T(8,128)(2,1)}, bf16[512,512]{1,0:T(8,128)(2,1)S(1)}, bf16[512,512]{1,0:T(8,128)(2,1)S(1)}, bf16[2048,256]{1,0:T(8,128)(2,1)S(1)}, bf16[2048,256]{1,0:T(8,128)(2,1)S(1)}) custom-call(s32[2]{0:T(128)S(1)} %copy-done.4, f32[2048,128]{1,0:T(8,128)} %bitcast.16, f32[2048,128]{1,0:T(8,128)} %bitcast.17, ...), custom_call_target="tpu_custom_call" | custom-call | tf_op jit(solution)/shard_map/pallas_call | solution.py:270
  38.3 0.0 copy-done
  38.3 0.0 copy-done.1
  38.3 0.0 copy-start.2
  38.3 1.6 %copy-done.2 = bf16[512,2048]{1,0:T(8,128)(2,1)S(1)} copy-done((bf16[512,2048]{1,0:T(8,128)(2,1)S(1)}, bf16[512,2048]{1,0:T(8,128)(2,1)}, u32[]{:S(2)}) %copy-start.2) | copy-done | bytes 2097176
  39.9 5.7 %shard_map.87 = (bf16[2,2048,256]{2,1,0:T(8,128)(2,1)}, bf16[2,2048,256]{2,1,0:T(8,128)(2,1)}) custom-call(bf16[512,2048]{1,0:T(8,128)(2,1)S(1)} %copy-done.2, bf16[512,512]{1,0:T(8,128)(2,1)S(1)} %get-tuple-element.10.high_ref, bf16[512,512]{1,0:T(8,128)(2,1)S(1)} %get-tuple-element.11.low_ref, bf16[2048,256]{1,0:T(8,128)(2,1)S(1)} %get-tuple-element.12.psi0_ref, ...), custom_call_target="tpu_custom_call" | custom-call | tf_op jit(solution)/shard_map/pallas_call | solution.py:324
Async XLA Ops:
  0.6 0.7 %copy-start.3 = (s32[1,256]{1,0:T(1,128)S(1)}, s32[1,256]{1,0:T(1,128)}, u32[]{:S(2)}) copy-start(s32[1,256]{1,0:T(1,128)} %kinetic_ref.1) | copy-start | bytes 3076
  1.3 0.7 %copy-start.4 = (s32[2]{0:T(128)S(1)}, s32[2]{0:T(128)}, u32[]{:S(2)}) copy-start(s32[2]{0:T(128)} %keepers_hbm.1) | copy-start | bytes 28
  2.0 36.3 %copy-start = (bf16[2,2048,1,256]{3,1,2,0:T(8,128)(2,1)S(1)}, bf16[2,2048,1,256]{3,1,2,0:T(8,128)(2,1)}, u32[]{:S(2)}) copy-start(bf16[2,2048,1,256]{3,1,2,0:T(8,128)(2,1)} %param.9) | copy-start | bytes 6291460
  2.0 36.3 %copy-start.1 = (bf16[2,2048,1,256]{3,1,2,0:T(8,128)(2,1)S(1)}, bf16[2,2048,1,256]{3,1,2,0:T(8,128)(2,1)}, u32[]{:S(2)}) copy-start(bf16[2,2048,1,256]{3,1,2,0:T(8,128)(2,1)} %param.10) | copy-start | bytes 6291460
  38.3 1.6 %copy-start.2 = (bf16[512,2048]{1,0:T(8,128)(2,1)S(1)}, bf16[512,2048]{1,0:T(8,128)(2,1)}, u32[]{:S(2)}) copy-start(bf16[512,2048]{1,0:T(8,128)(2,1)} %get-tuple-element.9.vmat_ref) | copy-start | bytes 6291460

commit v3 on v2

--- a/solution.py
+++ b/solution.py
@@ -12,6 +12,7 @@
 PARTS = 4
 TOP = 32766.0
 TILE = 256
+GRANT = 60 * 2**20
 MESH = pl.DeviceIdType.MESH
 
 
@@ -34,11 +35,11 @@
 
 def exchange_kernel(
     n, rows, chunks,
-    keepers_hbm, res_hbm, loc_hbm, store_hbm, kinetic_ref, psi_hbm, hpsi_hbm,
-    vmat_ref, high1_ref, low1_ref, psi0_ref, hpsi0_ref,
-    keepers, res, loc, masked, psi_sum, hpsi_sum,
-    out_codes, out_scales, codes, scales, chip_sum, far_sum, high0, low0,
-    load_sem, code_send, code_recv, scale_send, scale_recv,
+    keepers_hbm, res_hbm, loc_hbm, store_hbm, lattice_hbm, psi_hbm, hpsi_hbm,
+    vmat_out, high_out, low_out, psi0_out, hpsi0_out,
+    keepers, res, loc, masked, lattice, psi_sum, hpsi_sum, vmat_ref,
+    out_codes, out_scales, codes, scales, chip_sum, far_sum, high0, low0, high1, low1,
+    load_sem, store_sem, high_sem, low_sem, code_send, code_recv, scale_send, scale_recv,
     sib_send, sib_recv, far_send, far_recv, side_send, side_recv, back_send, back_recv,
 ):
     me = lax.axis_index("pw")
@@ -56,20 +57,24 @@
     own_start = pl.multiple_of(core * half, half)
     other_start = pl.multiple_of((1 - core) * half, half)
 
+    plane_rows = rows * chunks
     loads = [
         pltpu.make_async_copy(src, dst, load_sem.at[i])
         for i, (src, dst) in enumerate(
             (
+                (res_hbm.at[pl.ds(0, plane_rows)], res.at[pl.ds(0, plane_rows)]),
+                (loc_hbm.at[pl.ds(0, plane_rows)], loc.at[pl.ds(0, plane_rows)]),
                 (keepers_hbm, keepers),
-                (res_hbm, res),
-                (loc_hbm, loc),
                 (store_hbm, masked),
+                (res_hbm.at[pl.ds(plane_rows, plane_rows)], res.at[pl.ds(plane_rows, plane_rows)]),
+                (loc_hbm.at[pl.ds(plane_rows, plane_rows)], loc.at[pl.ds(plane_rows, plane_rows)]),
+                (lattice_hbm, lattice),
                 (psi_hbm.at[0], psi_sum),
                 (hpsi_hbm.at[0], hpsi_sum),
             )
         )
     ]
-    for load in loads[:4]:
+    for load in loads:
         load.start()
 
     barrier = pltpu.get_barrier_semaphore()
@@ -165,19 +170,24 @@
 
         return 0
 
-    def arrive(plane, k, _):
-        d = (me + n // 2 + k) % n
-
-        @pl.when(k != n // 2)
-        def _():
-            scale_copy(plane, k, d).wait()
-            code_copy(plane, k, d).wait()
-
-        return 0
-
-    def unpack(plane, high, low):
-        kinetic = kinetic_of(kinetic_ref[...])
-        group = max(1, 16 // rows)
+    group = max(1, 16 // rows)
+
+    def rows_copy(i, src, dst, sem):
+        at = pl.ds(pl.multiple_of(i * group * rows, group * rows), group * rows)
+        return pltpu.make_async_copy(src.at[at], dst.at[at], sem.at[i])
+
+    def receive(plane, high, low):
+        kinetic = kinetic_of(lattice[...])
+
+        def arrive(k, _):
+            d = (me + n // 2 + k) % n
+
+            @pl.when(k != n // 2)
+            def _():
+                scale_copy(plane, k, d).wait()
+                code_copy(plane, k, d).wait()
+
+            return 0
 
         def columns(s):
             q = codes[plane, s].astype(jnp.int32).astype(jnp.float32)
@@ -186,22 +196,37 @@
             other = q[rows:] * scale[1:2]
             return jnp.concatenate([corr, kinetic * corr + other], axis=1)
 
-        def step(i, _):
+        def unpack(i):
             both = jnp.concatenate([columns(i * group + j) for j in range(group)], axis=0)
             top = both.astype(jnp.bfloat16)
             at = pl.ds(pl.multiple_of(i * group * rows, group * rows), group * rows)
             high[at, :] = top
             low[at, :] = (both - top.astype(jnp.float32)).astype(jnp.bfloat16)
+            if plane == 1:
+                rows_copy(i, high, high_out, high_sem).start()
+                rows_copy(i, low, low_out, low_sem).start()
+
+        def in_turn(k, _):
+            arrive(k, 0)
+            unpack((me + 2 * n - n // 2 - k) % n)
             return 0
 
-        lax.fori_loop(0, n // group, step, 0)
-
+        def in_order(i, _):
+            unpack(i)
+            return 0
+
+        if group == 1:
+            lax.fori_loop(0, n, in_turn, 0)
+        else:
+            lax.fori_loop(0, n, arrive, 0)
+            lax.fori_loop(0, n // group, in_order, 0)
+
+    loads[0].wait()
     loads[1].wait()
-    loads[2].wait()
     pl.semaphore_wait(barrier, n + 1)
     lax.fori_loop(0, n // 2, functools.partial(send, 0), 0)
 
-    loads[0].wait()
+    loads[2].wait()
     loads[3].wait()
     for panel in range(2):
         keep = (keepers[panel] == band).astype(jnp.float32).astype(jnp.bfloat16)
@@ -216,9 +241,11 @@
     masked[mine, :] = masked[mine, :] + chip_sum[...]
     for i in range(3):
         far_copy(i, fetched[i]).start()
+    loads[4].wait()
+    loads[5].wait()
     lax.fori_loop(0, n, functools.partial(send, 1), 0)
-    for load in loads[4:]:
-        load.start()
+    for load in loads[6:]:
+        load.wait()
 
     for i in range(3):
         far_copy(i, fetched[i]).wait_recv()
@@ -232,28 +259,38 @@
     side_copy(fetched[3]).wait_recv()
     back_copy(3, own_start, fetched[3]).start()
 
-    lax.fori_loop(0, n, functools.partial(arrive, 0), 0)
-    unpack(0, high0, low0)
+    receive(0, high0, low0)
     for i in range(PARTS):
         back_copy(i, other_start, fetched[i]).wait_recv()
-    for load in loads[4:]:
-        load.wait()
+    stores = [
+        pltpu.make_async_copy(src, dst, store_sem.at[i])
+        for i, (src, dst) in enumerate(
+            ((vmat_ref, vmat_out), (psi_sum, psi0_out), (hpsi_sum, hpsi0_out))
+        )
+    ]
+    stores[0].start()
 
     def tile(j, _):
         at = pl.ds(pl.multiple_of(j * TILE, TILE), TILE)
         total = rotated(vmat_ref[:, at], high0[...], low0[...])
-        psi0_ref[at, :] = (psi_sum[at, :].astype(jnp.float32) + total[:, :cols]).astype(jnp.bfloat16)
-        hpsi0_ref[at, :] = (hpsi_sum[at, :].astype(jnp.float32) + total[:, cols:]).astype(jnp.bfloat16)
+        psi_sum[at, :] = (psi_sum[at, :].astype(jnp.float32) + total[:, :cols]).astype(jnp.bfloat16)
+        hpsi_sum[at, :] = (hpsi_sum[at, :].astype(jnp.float32) + total[:, cols:]).astype(jnp.bfloat16)
         return 0
 
     lax.fori_loop(0, vmat_ref.shape[1] // TILE, tile, 0)
-
-    lax.fori_loop(0, n, functools.partial(arrive, 1), 0)
-    unpack(1, high1_ref, low1_ref)
+    stores[1].start()
+    stores[2].start()
+
+    receive(1, high1, low1)
     for i in range(3):
         far_copy(i, fetched[i]).wait_send()
     for i in range(PARTS):
         back_copy(i, own_start, fetched[i]).wait_send()
+    for store in stores:
+        store.wait()
+    for i in range(n // group):
+        rows_copy(i, high1, high_out, high_sem).wait()
+        rows_copy(i, low1, low_out, low_sem).wait()
 
 
 def exchange(n, keepers, res, loc, store, lattice, psi, hpsi):
@@ -263,7 +300,6 @@
     cols = width // n
     flat = (planes * rows * chunks, LANES)
     dma = pltpu.SemaphoreType.DMA
-    vmem = pl.BlockSpec(memory_space=pltpu.VMEM)
     hbm = pl.BlockSpec(memory_space=pltpu.HBM)
     parts = jax.ShapeDtypeStruct((depth, 2 * cols), jnp.bfloat16)
     plane = jax.ShapeDtypeStruct((span, cols), jnp.bfloat16)
@@ -272,15 +308,17 @@
         out_shape=(
             jax.ShapeDtypeStruct((depth, span), jnp.bfloat16), parts, parts, plane, plane,
         ),
-        in_specs=[hbm, hbm, hbm, hbm, vmem, hbm, hbm],
-        out_specs=(vmem,) * 5,
+        in_specs=[hbm] * 7,
+        out_specs=(hbm,) * 5,
         scratch_shapes=[
             pltpu.SMEM((2,), jnp.int32),
             pltpu.VMEM(flat, jnp.float32),
             pltpu.VMEM(flat, jnp.float32),
             pltpu.VMEM((depth, span), jnp.bfloat16),
+            pltpu.VMEM(lattice.shape, jnp.int32),
             pltpu.VMEM((span, cols), jnp.bfloat16),
             pltpu.VMEM((span, cols), jnp.bfloat16),
+            pltpu.VMEM((depth, span), jnp.bfloat16),
             pltpu.VMEM((planes, n, 2 * rows, cols), jnp.int16),
             pltpu.VMEM((planes, n, 8, cols), jnp.float32),
             pltpu.VMEM((planes, n, 2 * rows, cols), jnp.int16),
@@ -289,12 +327,14 @@
             pltpu.VMEM((depth // 2, span), jnp.bfloat16),
             pltpu.VMEM((depth, 2 * cols), jnp.bfloat16),
             pltpu.VMEM((depth, 2 * cols), jnp.bfloat16),
-            dma((6,)), dma((planes, n)), dma((planes, n)), dma((planes, n)), dma((planes, n)),
+            pltpu.VMEM((depth, 2 * cols), jnp.bfloat16),
+            pltpu.VMEM((depth, 2 * cols), jnp.bfloat16),
+            dma((9,)), dma((3,)), dma((n,)), dma((n,)), dma((planes, n)), dma((planes, n)), dma((planes, n)), dma((planes, n)),
             dma((PARTS,)), dma((PARTS,)), dma((3,)), dma((3,)), dma, dma,
             dma((PARTS,)), dma((PARTS,)),
         ],
         compiler_params=pltpu.CompilerParams(
-            collective_id=0, has_side_effects=True, vmem_limit_bytes=50 * 2**20
+            collective_id=0, has_side_effects=True, vmem_limit_bytes=GRANT
         ),
     )(
         keepers, res.reshape(flat), loc.reshape(flat), store.reshape(depth, span),
@@ -303,34 +343,85 @@
 
 
 def rotate_kernel(
-    vmat_ref, high_ref, low_ref, psi0_ref, hpsi0_ref, psi_ref, hpsi_ref, psi_out, hpsi_out
+    vmat_hbm, high_hbm, low_hbm, psi0_hbm, hpsi0_hbm, psi_hbm, hpsi_hbm,
+    psi_out, hpsi_out,
+    vmat, high, low, psi, hpsi, load_sem, vmat_sem, plane_sem, psi_sem, hpsi_sem,
 ):
-    cols = psi0_ref.shape[1]
-    total = rotated(vmat_ref[...], high_ref[...], low_ref[...])
-    psi_out[0] = psi0_ref[...]
-    hpsi_out[0] = hpsi0_ref[...]
-    psi_out[1] = (psi_ref[0].astype(jnp.float32) + total[:, :cols]).astype(jnp.bfloat16)
-    hpsi_out[1] = (hpsi_ref[0].astype(jnp.float32) + total[:, cols:]).astype(jnp.bfloat16)
+    span, cols = psi.shape
+    tiles = span // TILE
+
+    def tile(j):
+        return pl.ds(pl.multiple_of(j * TILE, TILE), TILE)
+
+    def vmat_copy(j):
+        return pltpu.make_async_copy(
+            vmat_hbm.at[:, tile(j)], vmat.at[:, tile(j)], vmat_sem.at[j]
+        )
+
+    def out_copy(j, src, dst, sem):
+        return pltpu.make_async_copy(src.at[tile(j)], dst.at[1, tile(j)], sem.at[j])
+
+    loads = [
+        pltpu.make_async_copy(src, dst, load_sem.at[i])
+        for i, (src, dst) in enumerate(
+            ((high_hbm, high), (low_hbm, low), (psi_hbm.at[1], psi), (hpsi_hbm.at[1], hpsi))
+        )
+    ]
+    first = [
+        pltpu.make_async_copy(psi0_hbm, psi_out.at[0], plane_sem.at[0]),
+        pltpu.make_async_copy(hpsi0_hbm, hpsi_out.at[0], plane_sem.at[1]),
+    ]
+    loads[0].start()
+    loads[1].start()
+    vmat_copy(0).start()
+    loads[2].start()
+    loads[3].start()
+    for j in range(1, tiles):
+        vmat_copy(j).start()
+    for copy in first:
+        copy.start()
+    for load in loads:
+        load.wait()
+
+    def step(j, _):
+        vmat_copy(j).wait()
+        at = tile(j)
+        total = rotated(vmat[:, at], high[...], low[...])
+        psi[at, :] = (psi[at, :].astype(jnp.float32) + total[:, :cols]).astype(jnp.bfloat16)
+        hpsi[at, :] = (hpsi[at, :].astype(jnp.float32) + total[:, cols:]).astype(jnp.bfloat16)
+        out_copy(j, psi, psi_out, psi_sem).start()
+        out_copy(j, hpsi, hpsi_out, hpsi_sem).start()
+        return 0
+
+    lax.fori_loop(0, tiles, step, 0)
+    for j in range(tiles):
+        out_copy(j, psi, psi_out, psi_sem).wait()
+        out_copy(j, hpsi, hpsi_out, hpsi_sem).wait()
+    for copy in first:
+        copy.wait()
 
 
 def rotate(vmat, high, low, psi0, hpsi0, psi, hpsi):
     depth, span = vmat.shape
     cols = psi0.shape[1]
-    halves = pl.BlockSpec((depth, 2 * cols), lambda j: (0, 0))
-    done = pl.BlockSpec((TILE, cols), lambda j: (j, 0))
-    second = pl.BlockSpec((1, TILE, cols), lambda j: (1, j, 0))
-    band_tile = pl.BlockSpec((2, TILE, cols), lambda j: (0, j, 0))
+    tiles = span // TILE
+    dma = pltpu.SemaphoreType.DMA
+    hbm = pl.BlockSpec(memory_space=pltpu.HBM)
     out = jax.ShapeDtypeStruct((2, span, cols), jnp.bfloat16)
     return pl.pallas_call(
         rotate_kernel,
-        grid=(span // TILE,),
         out_shape=(out, out),
-        in_specs=[
-            pl.BlockSpec((depth, TILE), lambda j: (0, j)),
-            halves, halves, done, done, second, second,
+        in_specs=[hbm] * 7,
+        out_specs=(hbm, hbm),
+        scratch_shapes=[
+            pltpu.VMEM((depth, span), jnp.bfloat16),
+            pltpu.VMEM((depth, 2 * cols), jnp.bfloat16),
+            pltpu.VMEM((depth, 2 * cols), jnp.bfloat16),
+            pltpu.VMEM((span, cols), jnp.bfloat16),
+            pltpu.VMEM((span, cols), jnp.bfloat16),
+            dma((4,)), dma((tiles,)), dma((2,)), dma((tiles,)), dma((tiles,)),
         ],
-        out_specs=(band_tile, band_tile),
-        compiler_params=pltpu.CompilerParams(vmem_limit_bytes=40 * 2**20),
+        compiler_params=pltpu.CompilerParams(vmem_limit_bytes=GRANT),
     )(vmat, high, low, psi0, hpsi0, psi, hpsi)
 
 

time: 46 us -> 102 us (2.22)
  Pallas kernels: 42 us -> 101 us
  local copies, waits for them, and re-layouts: 2.92 us -> 0 us
    pallas_call x1, Pallas kernels: 5.68 us -> 64.9 us  [rotate(): pl.pallas_call(rotate_kernel, out_shape=(out, out), in_specs=[hbm] * 7, o...]
    unnamed x10 -> x0, local copies, waits for them, and re-layouts: 2.92 us -> none
where the time goes in v3:
time: 102 us
  Pallas kernels  101 us (99%)
    pallas_call x1, Pallas kernels, rotate(): pl.pallas_call(rotate_kernel, out_shape=(out, out), in_specs=[hbm] * 7, o...  64.9 us
    pallas_call x1, Pallas kernels, exchange(): pl.pallas_call(functools.partial(exchange_kernel, n, rows, chunks), out_s...  36.4 us

profile of v3, /device:TPU:0, one launch (start us, length us, event | category | flops | bytes accessed | tf_op | source)
XLA Modules:
  0.0 102.0 jit_solution(13471589539631677501)
XLA Ops:
  0.6 36.4 %shard_map.86 = (bf16[512,2048]{1,0:T(8,128)(2,1)}, bf16[512,512]{1,0:T(8,128)(2,1)}, bf16[512,512]{1,0:T(8,128)(2,1)}, bf16[2048,256]{1,0:T(8,128)(2,1)}, bf16[2048,256]{1,0:T(8,128)(2,1)}) custom-call(s32[2]{0:T(128)} %keepers_hbm.1, f32[2048,128]{1,0:T(8,128)} %bitcast.16, f32[2048,128]{1,0:T(8,128)} %bitcast.17, bf16[512,2048]{1,0:T(8,128)(2,1)} %bitcast.15, ...), custom_call_target="tpu_custom_call" | custom-call | tf_op jit(solution)/shard_map/pallas_call | solution.py:306
  37.1 64.9 %shard_map.87 = (bf16[2,2048,256]{2,1,0:T(8,128)(2,1)}, bf16[2,2048,256]{2,1,0:T(8,128)(2,1)}) custom-call(bf16[512,2048]{1,0:T(8,128)(2,1)} %get-tuple-element.9.vmat_hbm, bf16[512,512]{1,0:T(8,128)(2,1)} %get-tuple-element.10.high_hbm, bf16[512,512]{1,0:T(8,128)(2,1)} %get-tuple-element.11.low_hbm, bf16[2048,256]{1,0:T(8,128)(2,1)} %get-tuple-element.12.psi0_hbm, ...), custom_call_target="tpu_custom_call" | custom-call | tf_op jit(solution)/shard_map/pallas_call | solution.py:411

commit v4 on v3

--- a/solution.py
+++ b/solution.py
@@ -58,16 +58,19 @@
     other_start = pl.multiple_of((1 - core) * half, half)
 
     plane_rows = rows * chunks
+    first, second = pl.ds(0, plane_rows), pl.ds(plane_rows, plane_rows)
+    other, mine = pl.ds(other_start, half), pl.ds(own_start, half)
     loads = [
         pltpu.make_async_copy(src, dst, load_sem.at[i])
         for i, (src, dst) in enumerate(
             (
-                (res_hbm.at[pl.ds(0, plane_rows)], res.at[pl.ds(0, plane_rows)]),
-                (loc_hbm.at[pl.ds(0, plane_rows)], loc.at[pl.ds(0, plane_rows)]),
                 (keepers_hbm, keepers),
-                (store_hbm, masked),
-                (res_hbm.at[pl.ds(plane_rows, plane_rows)], res.at[pl.ds(plane_rows, plane_rows)]),
-                (loc_hbm.at[pl.ds(plane_rows, plane_rows)], loc.at[pl.ds(plane_rows, plane_rows)]),
+                (store_hbm.at[other], masked.at[other]),
+                (res_hbm.at[first], res.at[first]),
+                (loc_hbm.at[first], loc.at[first]),
+                (store_hbm.at[mine], masked.at[mine]),
+                (res_hbm.at[second], res.at[second]),
+                (loc_hbm.at[second], loc.at[second]),
                 (lattice_hbm, lattice),
                 (psi_hbm.at[0], psi_sum),
                 (hpsi_hbm.at[0], hpsi_sum),
@@ -89,11 +92,11 @@
         pl.semaphore_signal(barrier, inc=1, device_id={"band": peer}, device_id_type=MESH)
     out_scales[...] = jnp.zeros_like(out_scales)
 
-    def sib_copy(q):
+    def sib_copy(i, q):
         return pltpu.make_async_remote_copy(
             src_ref=masked.at[pl.ds(other_start + q * part, part)],
             dst_ref=chip_sum.at[pl.ds(q * part, part)],
-            send_sem=sib_send.at[q], recv_sem=sib_recv.at[q],
+            send_sem=sib_send.at[i], recv_sem=sib_recv.at[i],
             device_id={"band": sibling}, device_id_type=MESH,
         )
 
@@ -221,30 +224,31 @@
             lax.fori_loop(0, n, arrive, 0)
             lax.fori_loop(0, n // group, in_order, 0)
 
+    def keep(panel):
+        return (keepers[panel] == band).astype(jnp.float32).astype(jnp.bfloat16)
+
     loads[0].wait()
     loads[1].wait()
     pl.semaphore_wait(barrier, n + 1)
-    lax.fori_loop(0, n // 2, functools.partial(send, 0), 0)
-
+    for i in range(3):
+        at = pl.ds(pl.multiple_of(other_start + fetched[i] * part, part), part)
+        masked[at, :] = masked[at, :] * keep(1 - core)
+        sib_copy(i, fetched[i]).start()
     loads[2].wait()
     loads[3].wait()
-    for panel in range(2):
-        keep = (keepers[panel] == band).astype(jnp.float32).astype(jnp.bfloat16)
-        at = pl.ds(panel * half, half)
-        masked[at, :] = masked[at, :] * keep
-    for q in range(PARTS):
-        sib_copy(q).start()
+    lax.fori_loop(0, n // 2, functools.partial(send, 0), 0)
+    loads[4].wait()
+    for i in range(3):
+        sib_copy(i, fetched[i]).wait_recv()
+        at = pl.ds(pl.multiple_of(own_start + fetched[i] * part, part), part)
+        near = pl.ds(pl.multiple_of(fetched[i] * part, part), part)
+        masked[at, :] = masked[at, :] * keep(core) + chip_sum[near, :]
+        far_copy(i, fetched[i]).start()
     lax.fori_loop(n // 2, n, functools.partial(send, 0), 0)
-    for q in range(PARTS):
-        sib_copy(q).wait()
-    mine = pl.ds(own_start, half)
-    masked[mine, :] = masked[mine, :] + chip_sum[...]
-    for i in range(3):
-        far_copy(i, fetched[i]).start()
-    loads[4].wait()
     loads[5].wait()
+    loads[6].wait()
     lax.fori_loop(0, n, functools.partial(send, 1), 0)
-    for load in loads[6:]:
+    for load in loads[7:]:
         load.wait()
 
     for i in range(3):
@@ -283,6 +287,7 @@
 
     receive(1, high1, low1)
     for i in range(3):
+        sib_copy(i, fetched[i]).wait_send()
         far_copy(i, fetched[i]).wait_send()
     for i in range(PARTS):
         back_copy(i, own_start, fetched[i]).wait_send()
@@ -329,8 +334,8 @@
             pltpu.VMEM((depth, 2 * cols), jnp.bfloat16),
             pltpu.VMEM((depth, 2 * cols), jnp.bfloat16),
             pltpu.VMEM((depth, 2 * cols), jnp.bfloat16),
-            dma((9,)), dma((3,)), dma((n,)), dma((n,)), dma((planes, n)), dma((planes, n)), dma((planes, n)), dma((planes, n)),
-            dma((PARTS,)), dma((PARTS,)), dma((3,)), dma((3,)), dma, dma,
+            dma((10,)), dma((3,)), dma((n,)), dma((n,)), dma((planes, n)), dma((planes, n)), dma((planes, n)), dma((planes, n)),
+            dma((3,)), dma((3,)), dma((3,)), dma((3,)), dma, dma,
             dma((PARTS,)), dma((PARTS,)),
         ],
         compiler_params=pltpu.CompilerParams(
@@ -345,7 +350,8 @@
 def rotate_kernel(
     vmat_hbm, high_hbm, low_hbm, psi0_hbm, hpsi0_hbm, psi_hbm, hpsi_hbm,
     psi_out, hpsi_out,
-    vmat, high, low, psi, hpsi, load_sem, vmat_sem, plane_sem, psi_sem, hpsi_sem,
+    vmat, high, low, psi, hpsi, psi0, hpsi0,
+    load_sem, vmat_sem, plane_sem, psi_sem, hpsi_sem,
 ):
     span, cols = psi.shape
     tiles = span // TILE
@@ -364,12 +370,19 @@
     loads = [
         pltpu.make_async_copy(src, dst, load_sem.at[i])
         for i, (src, dst) in enumerate(
-            ((high_hbm, high), (low_hbm, low), (psi_hbm.at[1], psi), (hpsi_hbm.at[1], hpsi))
+            (
+                (high_hbm, high),
+                (low_hbm, low),
+                (psi_hbm.at[1], psi),
+                (hpsi_hbm.at[1], hpsi),
+                (psi0_hbm, psi0),
+                (hpsi0_hbm, hpsi0),
+            )
         )
     ]
     first = [
-        pltpu.make_async_copy(psi0_hbm, psi_out.at[0], plane_sem.at[0]),
-        pltpu.make_async_copy(hpsi0_hbm, hpsi_out.at[0], plane_sem.at[1]),
+        pltpu.make_async_copy(psi0, psi_out.at[0], plane_sem.at[0]),
+        pltpu.make_async_copy(hpsi0, hpsi_out.at[0], plane_sem.at[1]),
     ]
     loads[0].start()
     loads[1].start()
@@ -378,9 +391,9 @@
     loads[3].start()
     for j in range(1, tiles):
         vmat_copy(j).start()
-    for copy in first:
-        copy.start()
-    for load in loads:
+    loads[4].start()
+    loads[5].start()
+    for load in loads[:4]:
         load.wait()
 
     def step(j, _):
@@ -393,7 +406,11 @@
         out_copy(j, hpsi, hpsi_out, hpsi_sem).start()
         return 0
 
-    lax.fori_loop(0, tiles, step, 0)
+    lax.fori_loop(0, tiles // 2, step, 0)
+    for i in range(2):
+        loads[4 + i].wait()
+        first[i].start()
+    lax.fori_loop(tiles // 2, tiles, step, 0)
     for j in range(tiles):
         out_copy(j, psi, psi_out, psi_sem).wait()
         out_copy(j, hpsi, hpsi_out, hpsi_sem).wait()
@@ -419,7 +436,9 @@
             pltpu.VMEM((depth, 2 * cols), jnp.bfloat16),
             pltpu.VMEM((span, cols), jnp.bfloat16),
             pltpu.VMEM((span, cols), jnp.bfloat16),
-            dma((4,)), dma((tiles,)), dma((2,)), dma((tiles,)), dma((tiles,)),
+            pltpu.VMEM((span, cols), jnp.bfloat16),
+            pltpu.VMEM((span, cols), jnp.bfloat16),
+            dma((6,)), dma((tiles,)), dma((2,)), dma((tiles,)), dma((tiles,)),
         ],
         compiler_params=pltpu.CompilerParams(vmem_limit_bytes=GRANT),
     )(vmat, high, low, psi0, hpsi0, psi, hpsi)

time: 102 us -> 42.5 us (0.42)
  Pallas kernels: 101 us -> 41.7 us
    pallas_call x1, Pallas kernels: 64.9 us -> 7.06 us  [rotate(): pl.pallas_call(rotate_kernel, out_shape=(out, out), in_specs=[hbm] * 7, o...]
    pallas_call x1, Pallas kernels: 36.4 us -> 34.7 us  [exchange(): pl.pallas_call(functools.partial(exchange_kernel, n, rows, chunks), out_s...]
where the time goes in v4:
time: 42.5 us; the launch traced here: 42.4 us
  Pallas kernels  41.7 us (98%)
  between operations  0.64 us (2%)
    pallas_call x1, Pallas kernels, exchange(): pl.pallas_call(functools.partial(exchange_kernel, n, rows, chunks), out_s...  34.7 us
    pallas_call x1, Pallas kernels, rotate(): pl.pallas_call(rotate_kernel, out_shape=(out, out), in_specs=[hbm] * 7, o...  7.06 us

profile of v4, /device:TPU:0, one launch (start us, length us, event | category | flops | bytes accessed | tf_op | source)
XLA Modules:
  0.0 42.4 jit_solution(1706975161259041125)
XLA Ops:
  0.6 34.7 %shard_map.86 = (bf16[512,2048]{1,0:T(8,128)(2,1)}, bf16[512,512]{1,0:T(8,128)(2,1)}, bf16[512,512]{1,0:T(8,128)(2,1)}, bf16[2048,256]{1,0:T(8,128)(2,1)}, bf16[2048,256]{1,0:T(8,128)(2,1)}) custom-call(s32[2]{0:T(128)} %keepers_hbm.1, f32[2048,128]{1,0:T(8,128)} %bitcast.16, f32[2048,128]{1,0:T(8,128)} %bitcast.17, bf16[512,2048]{1,0:T(8,128)(2,1)} %bitcast.15, ...), custom_call_target="tpu_custom_call" | custom-call | tf_op jit(solution)/shard_map/pallas_call | solution.py:311
  35.3 7.1 %shard_map.87 = (bf16[2,2048,256]{2,1,0:T(8,128)(2,1)}, bf16[2,2048,256]{2,1,0:T(8,128)(2,1)}) custom-call(bf16[512,2048]{1,0:T(8,128)(2,1)} %get-tuple-element.9.vmat_hbm, bf16[512,512]{1,0:T(8,128)(2,1)} %get-tuple-element.10.high_hbm, bf16[512,512]{1,0:T(8,128)(2,1)} %get-tuple-element.11.low_hbm, bf16[2048,256]{1,0:T(8,128)(2,1)} %get-tuple-element.12.psi0_hbm, ...), custom_call_target="tpu_custom_call" | custom-call | tf_op jit(solution)/shard_map/pallas_call | solution.py:428

commit v5 on v4

--- a/solution.py
+++ b/solution.py
@@ -11,7 +11,7 @@
 LANES = 128
 PARTS = 4
 TOP = 32766.0
-TILE = 256
+TILE = 512
 GRANT = 60 * 2**20
 MESH = pl.DeviceIdType.MESH
 
@@ -27,19 +27,20 @@
     return total.astype(jnp.float32) / (GRID * GRID)
 
 
-def rotated(v, high, low):
+def rotated(v, pieces):
     dims = (((0,), (0,)), ((), ()))
-    total = lax.dot_general(v, high, dims, preferred_element_type=jnp.float32)
-    return total + lax.dot_general(v, low, dims, preferred_element_type=jnp.float32)
+    total = lax.dot_general(v, pieces, dims, preferred_element_type=jnp.float32)
+    width = total.shape[1] // 2
+    return total[:, :width] + total[:, width:]
 
 
 def exchange_kernel(
     n, rows, chunks,
     keepers_hbm, res_hbm, loc_hbm, store_hbm, lattice_hbm, psi_hbm, hpsi_hbm,
-    vmat_out, high_out, low_out, psi0_out, hpsi0_out,
+    vmat_out, pieces_out, psi0_out, hpsi0_out,
     keepers, res, loc, masked, lattice, psi_sum, hpsi_sum, vmat_ref,
-    out_codes, out_scales, codes, scales, chip_sum, far_sum, high0, low0, high1, low1,
-    load_sem, store_sem, high_sem, low_sem, code_send, code_recv, scale_send, scale_recv,
+    out_codes, out_scales, codes, scales, chip_sum, far_sum, pieces0, pieces1,
+    load_sem, store_sem, pieces_sem, code_send, code_recv, scale_send, scale_recv,
     sib_send, sib_recv, far_send, far_recv, side_send, side_recv, back_send, back_recv,
 ):
     me = lax.axis_index("pw")
@@ -175,11 +176,11 @@
 
     group = max(1, 16 // rows)
 
-    def rows_copy(i, src, dst, sem):
+    def rows_copy(i):
         at = pl.ds(pl.multiple_of(i * group * rows, group * rows), group * rows)
-        return pltpu.make_async_copy(src.at[at], dst.at[at], sem.at[i])
-
-    def receive(plane, high, low):
+        return pltpu.make_async_copy(pieces1.at[at], pieces_out.at[at], pieces_sem.at[i])
+
+    def receive(plane, pieces):
         kinetic = kinetic_of(lattice[...])
 
         def arrive(k, _):
@@ -203,11 +204,10 @@
             both = jnp.concatenate([columns(i * group + j) for j in range(group)], axis=0)
             top = both.astype(jnp.bfloat16)
             at = pl.ds(pl.multiple_of(i * group * rows, group * rows), group * rows)
-            high[at, :] = top
-            low[at, :] = (both - top.astype(jnp.float32)).astype(jnp.bfloat16)
+            pieces[at, : 2 * cols] = top
+            pieces[at, 2 * cols :] = (both - top.astype(jnp.float32)).astype(jnp.bfloat16)
             if plane == 1:
-                rows_copy(i, high, high_out, high_sem).start()
-                rows_copy(i, low, low_out, low_sem).start()
+                rows_copy(i).start()
 
         def in_turn(k, _):
             arrive(k, 0)
@@ -263,7 +263,7 @@
     side_copy(fetched[3]).wait_recv()
     back_copy(3, own_start, fetched[3]).start()
 
-    receive(0, high0, low0)
+    receive(0, pieces0)
     for i in range(PARTS):
         back_copy(i, other_start, fetched[i]).wait_recv()
     stores = [
@@ -276,7 +276,7 @@
 
     def tile(j, _):
         at = pl.ds(pl.multiple_of(j * TILE, TILE), TILE)
-        total = rotated(vmat_ref[:, at], high0[...], low0[...])
+        total = rotated(vmat_ref[:, at], pieces0[...])
         psi_sum[at, :] = (psi_sum[at, :].astype(jnp.float32) + total[:, :cols]).astype(jnp.bfloat16)
         hpsi_sum[at, :] = (hpsi_sum[at, :].astype(jnp.float32) + total[:, cols:]).astype(jnp.bfloat16)
         return 0
@@ -285,7 +285,7 @@
     stores[1].start()
     stores[2].start()
 
-    receive(1, high1, low1)
+    receive(1, pieces1)
     for i in range(3):
         sib_copy(i, fetched[i]).wait_send()
         far_copy(i, fetched[i]).wait_send()
@@ -294,8 +294,7 @@
     for store in stores:
         store.wait()
     for i in range(n // group):
-        rows_copy(i, high1, high_out, high_sem).wait()
-        rows_copy(i, low1, low_out, low_sem).wait()
+        rows_copy(i).wait()
 
 
 def exchange(n, keepers, res, loc, store, lattice, psi, hpsi):
@@ -306,15 +305,15 @@
     flat = (planes * rows * chunks, LANES)
     dma = pltpu.SemaphoreType.DMA
     hbm = pl.BlockSpec(memory_space=pltpu.HBM)
-    parts = jax.ShapeDtypeStruct((depth, 2 * cols), jnp.bfloat16)
+    parts = jax.ShapeDtypeStruct((depth, 4 * cols), jnp.bfloat16)
     plane = jax.ShapeDtypeStruct((span, cols), jnp.bfloat16)
     return pl.pallas_call(
         functools.partial(exchange_kernel, n, rows, chunks),
         out_shape=(
-            jax.ShapeDtypeStruct((depth, span), jnp.bfloat16), parts, parts, plane, plane,
+            jax.ShapeDtypeStruct((depth, span), jnp.bfloat16), parts, plane, plane,
         ),
         in_specs=[hbm] * 7,
-        out_specs=(hbm,) * 5,
+        out_specs=(hbm,) * 4,
         scratch_shapes=[
             pltpu.SMEM((2,), jnp.int32),
             pltpu.VMEM(flat, jnp.float32),
@@ -330,11 +329,9 @@
             pltpu.VMEM((planes, n, 8, cols), jnp.float32),
             pltpu.VMEM((depth // 2, span), jnp.bfloat16),
             pltpu.VMEM((depth // 2, span), jnp.bfloat16),
-            pltpu.VMEM((depth, 2 * cols), jnp.bfloat16),
-            pltpu.VMEM((depth, 2 * cols), jnp.bfloat16),
-            pltpu.VMEM((depth, 2 * cols), jnp.bfloat16),
-            pltpu.VMEM((depth, 2 * cols), jnp.bfloat16),
-            dma((10,)), dma((3,)), dma((n,)), dma((n,)), dma((planes, n)), dma((planes, n)), dma((planes, n)), dma((planes, n)),
+            pltpu.VMEM((depth, 4 * cols), jnp.bfloat16),
+            pltpu.VMEM((depth, 4 * cols), jnp.bfloat16),
+            dma((10,)), dma((3,)), dma((n,)), dma((planes, n)), dma((planes, n)), dma((planes, n)), dma((planes, n)),
             dma((3,)), dma((3,)), dma((3,)), dma((3,)), dma, dma,
             dma((PARTS,)), dma((PARTS,)),
         ],
@@ -348,10 +345,10 @@
 
 
 def rotate_kernel(
-    vmat_hbm, high_hbm, low_hbm, psi0_hbm, hpsi0_hbm, psi_hbm, hpsi_hbm,
+    vmat_hbm, pieces_hbm, psi0_hbm, hpsi0_hbm, psi_hbm, hpsi_hbm,
     psi_out, hpsi_out,
-    vmat, high, low, psi, hpsi, psi0, hpsi0,
-    load_sem, vmat_sem, plane_sem, psi_sem, hpsi_sem,
+    vmat, pieces, psi, hpsi, psi0, hpsi0,
+    pieces_sem, vmat_sem, psi_sem, hpsi_sem, psi_out_sem, hpsi_out_sem, first_sem, first_out_sem,
 ):
     span, cols = psi.shape
     tiles = span // TILE
@@ -359,98 +356,91 @@
     def tile(j):
         return pl.ds(pl.multiple_of(j * TILE, TILE), TILE)
 
-    def vmat_copy(j):
-        return pltpu.make_async_copy(
-            vmat_hbm.at[:, tile(j)], vmat.at[:, tile(j)], vmat_sem.at[j]
-        )
-
-    def out_copy(j, src, dst, sem):
-        return pltpu.make_async_copy(src.at[tile(j)], dst.at[1, tile(j)], sem.at[j])
-
-    loads = [
-        pltpu.make_async_copy(src, dst, load_sem.at[i])
-        for i, (src, dst) in enumerate(
-            (
-                (high_hbm, high),
-                (low_hbm, low),
-                (psi_hbm.at[1], psi),
-                (hpsi_hbm.at[1], hpsi),
-                (psi0_hbm, psi0),
-                (hpsi0_hbm, hpsi0),
-            )
-        )
-    ]
-    first = [
-        pltpu.make_async_copy(psi0, psi_out.at[0], plane_sem.at[0]),
-        pltpu.make_async_copy(hpsi0, hpsi_out.at[0], plane_sem.at[1]),
-    ]
-    loads[0].start()
-    loads[1].start()
-    vmat_copy(0).start()
-    loads[2].start()
-    loads[3].start()
-    for j in range(1, tiles):
-        vmat_copy(j).start()
-    loads[4].start()
-    loads[5].start()
-    for load in loads[:4]:
-        load.wait()
-
-    def step(j, _):
-        vmat_copy(j).wait()
+    def loads(j):
         at = tile(j)
-        total = rotated(vmat[:, at], high[...], low[...])
+        return (
+            pltpu.make_async_copy(vmat_hbm.at[:, at], vmat.at[:, at], vmat_sem.at[j]),
+            pltpu.make_async_copy(psi_hbm.at[1, at], psi.at[at], psi_sem.at[j]),
+            pltpu.make_async_copy(hpsi_hbm.at[1, at], hpsi.at[at], hpsi_sem.at[j]),
+        )
+
+    def stores(j):
+        at = tile(j)
+        return (
+            pltpu.make_async_copy(psi.at[at], psi_out.at[1, at], psi_out_sem.at[j]),
+            pltpu.make_async_copy(hpsi.at[at], hpsi_out.at[1, at], hpsi_out_sem.at[j]),
+        )
+
+    load_pieces = pltpu.make_async_copy(pieces_hbm, pieces, pieces_sem)
+    first_in = (
+        pltpu.make_async_copy(psi0_hbm, psi0, first_sem.at[0]),
+        pltpu.make_async_copy(hpsi0_hbm, hpsi0, first_sem.at[1]),
+    )
+    first_out = (
+        pltpu.make_async_copy(psi0, psi_out.at[0], first_out_sem.at[0]),
+        pltpu.make_async_copy(hpsi0, hpsi_out.at[0], first_out_sem.at[1]),
+    )
+    load_pieces.start()
+    for load in loads(0) + loads(1):
+        load.start()
+    for load in first_in:
+        load.start()
+    for j in range(2, tiles):
+        for load in loads(j):
+            load.start()
+    load_pieces.wait()
+
+    for j in range(tiles):
+        for load in loads(j):
+            load.wait()
+        at = tile(j)
+        total = rotated(vmat[:, at], pieces[...])
         psi[at, :] = (psi[at, :].astype(jnp.float32) + total[:, :cols]).astype(jnp.bfloat16)
         hpsi[at, :] = (hpsi[at, :].astype(jnp.float32) + total[:, cols:]).astype(jnp.bfloat16)
-        out_copy(j, psi, psi_out, psi_sem).start()
-        out_copy(j, hpsi, hpsi_out, hpsi_sem).start()
-        return 0
-
-    lax.fori_loop(0, tiles // 2, step, 0)
-    for i in range(2):
-        loads[4 + i].wait()
-        first[i].start()
-    lax.fori_loop(tiles // 2, tiles, step, 0)
+        for store in stores(j):
+            store.start()
+        if j == 0:
+            for i in range(2):
+                first_in[i].wait()
+                first_out[i].start()
     for j in range(tiles):
-        out_copy(j, psi, psi_out, psi_sem).wait()
-        out_copy(j, hpsi, hpsi_out, hpsi_sem).wait()
-    for copy in first:
-        copy.wait()
-
-
-def rotate(vmat, high, low, psi0, hpsi0, psi, hpsi):
+        for store in stores(j):
+            store.wait()
+    for store in first_out:
+        store.wait()
+
+
+def rotate(vmat, pieces, psi0, hpsi0, psi, hpsi):
     depth, span = vmat.shape
     cols = psi0.shape[1]
     tiles = span // TILE
     dma = pltpu.SemaphoreType.DMA
     hbm = pl.BlockSpec(memory_space=pltpu.HBM)
     out = jax.ShapeDtypeStruct((2, span, cols), jnp.bfloat16)
+    plane = pltpu.VMEM((span, cols), jnp.bfloat16)
     return pl.pallas_call(
         rotate_kernel,
         out_shape=(out, out),
-        in_specs=[hbm] * 7,
+        in_specs=[hbm] * 6,
         out_specs=(hbm, hbm),
         scratch_shapes=[
             pltpu.VMEM((depth, span), jnp.bfloat16),
-            pltpu.VMEM((depth, 2 * cols), jnp.bfloat16),
-            pltpu.VMEM((depth, 2 * cols), jnp.bfloat16),
-            pltpu.VMEM((span, cols), jnp.bfloat16),
-            pltpu.VMEM((span, cols), jnp.bfloat16),
-            pltpu.VMEM((span, cols), jnp.bfloat16),
-            pltpu.VMEM((span, cols), jnp.bfloat16),
-            dma((6,)), dma((tiles,)), dma((2,)), dma((tiles,)), dma((tiles,)),
+            pltpu.VMEM((depth, 4 * cols), jnp.bfloat16),
+            plane, plane, plane, plane,
+            dma, dma((tiles,)), dma((tiles,)), dma((tiles,)), dma((tiles,)), dma((tiles,)),
+            dma((2,)), dma((2,)),
         ],
         compiler_params=pltpu.CompilerParams(vmem_limit_bytes=GRANT),
-    )(vmat, high, low, psi0, hpsi0, psi, hpsi)
+    )(vmat, pieces, psi0, hpsi0, psi, hpsi)
 
 
 def per_device(n, res, loc, psi, hpsi, store, keepers, lattice):
     planes, span, _, cols = psi.shape
     psi_in, hpsi_in = (x.reshape(planes, span, cols) for x in (psi, hpsi))
-    vmat, high, low, psi0, hpsi0 = exchange(
+    vmat, pieces, psi0, hpsi0 = exchange(
         n, keepers, res, loc, store, lattice, psi_in, hpsi_in
     )
-    psi_new, hpsi_new = rotate(vmat, high, low, psi0, hpsi0, psi_in, hpsi_in)
+    psi_new, hpsi_new = rotate(vmat, pieces, psi0, hpsi0, psi_in, hpsi_in)
     return psi_new.reshape(psi.shape), hpsi_new.reshape(hpsi.shape)
 
 

time: 42.5 us -> 41.6 us (0.979)
  Pallas kernels: 41.7 us -> 40.8 us
    pallas_call x1, Pallas kernels: 7.06 us -> 6.52 us  [rotate(): pl.pallas_call(rotate_kernel, out_shape=(out, out), in_specs=[hbm] * 6, o...]
where the time goes in v5:
time: 41.6 us; the launch traced here: 41.4 us
  Pallas kernels  40.8 us (98%)
  between operations  0.64 us (2%)
    pallas_call x1, Pallas kernels, exchange(): pl.pallas_call(functools.partial(exchange_kernel, n, rows, chunks), out_s...  34.3 us
    pallas_call x1, Pallas kernels, rotate(): pl.pallas_call(rotate_kernel, out_shape=(out, out), in_specs=[hbm] * 6, o...  6.52 us

profile of v5, /device:TPU:0, one launch (start us, length us, event | category | flops | bytes accessed | tf_op | source)
XLA Modules:
  0.0 41.4 jit_solution(13862258533545154277)
XLA Ops:
  0.6 34.3 %shard_map.86 = (bf16[512,2048]{1,0:T(8,128)(2,1)}, bf16[512,1024]{1,0:T(8,128)(2,1)}, bf16[2048,256]{1,0:T(8,128)(2,1)}, bf16[2048,256]{1,0:T(8,128)(2,1)}) custom-call(s32[2]{0:T(128)} %keepers_hbm.1, f32[2048,128]{1,0:T(8,128)} %bitcast.16, f32[2048,128]{1,0:T(8,128)} %bitcast.17, bf16[512,2048]{1,0:T(8,128)(2,1)} %bitcast.15, s32[1,256]{1,0:T(1,128)} %lattice_hbm.1, ...), custom_call_target="tpu_custom_call" | custom-call | tf_op jit(solution)/shard_map/pallas_call | solution.py:310
  34.9 6.5 %shard_map.87 = (bf16[2,2048,256]{2,1,0:T(8,128)(2,1)}, bf16[2,2048,256]{2,1,0:T(8,128)(2,1)}) custom-call(bf16[512,2048]{1,0:T(8,128)(2,1)} %get-tuple-element.8.vmat_hbm, bf16[512,1024]{1,0:T(8,128)(2,1)} %get-tuple-element.9.pieces_hbm, bf16[2048,256]{1,0:T(8,128)(2,1)} %get-tuple-element.10.psi0_hbm, bf16[2048,256]{1,0:T(8,128)(2,1)} %get-tuple-element.11.hpsi0_hbm, ...), custom_call_target="tpu_custom_call" | custom-call | tf_op jit(solution)/shard_map/pallas_call | solution.py:421

commit v6 on v5

--- a/solution.py
+++ b/solution.py
@@ -12,7 +12,7 @@
 PARTS = 4
 TOP = 32766.0
 TILE = 512
-GRANT = 60 * 2**20
+GRANT = 52 * 2**20
 MESH = pl.DeviceIdType.MESH
 
 
@@ -37,10 +37,10 @@
 def exchange_kernel(
     n, rows, chunks,
     keepers_hbm, res_hbm, loc_hbm, store_hbm, lattice_hbm, psi_hbm, hpsi_hbm,
-    vmat_out, pieces_out, psi0_out, hpsi0_out,
-    keepers, res, loc, masked, lattice, psi_sum, hpsi_sum, vmat_ref,
-    out_codes, out_scales, codes, scales, chip_sum, far_sum, pieces0, pieces1,
-    load_sem, store_sem, pieces_sem, code_send, code_recv, scale_send, scale_recv,
+    vmat_out, pieces1, psi_sum, hpsi_sum, psi1, hpsi1,
+    keepers, res, loc, masked, lattice, vmat_ref,
+    out_codes, out_scales, codes, scales, chip_sum, far_sum, pieces0,
+    load_sem, store_sem, code_send, code_recv, scale_send, scale_recv,
     sib_send, sib_recv, far_send, far_recv, side_send, side_recv, back_send, back_recv,
 ):
     me = lax.axis_index("pw")
@@ -75,6 +75,8 @@
                 (lattice_hbm, lattice),
                 (psi_hbm.at[0], psi_sum),
                 (hpsi_hbm.at[0], hpsi_sum),
+                (psi_hbm.at[1], psi1),
+                (hpsi_hbm.at[1], hpsi1),
             )
         )
     ]
@@ -169,16 +171,14 @@
 
         @pl.when(k != n // 2)
         def _():
+            if plane == 1:
+                code_copy(0, k, d).wait_send()
             scale_copy(plane, k, d).start()
             code_copy(plane, k, d).start()
 
         return 0
 
     group = max(1, 16 // rows)
-
-    def rows_copy(i):
-        at = pl.ds(pl.multiple_of(i * group * rows, group * rows), group * rows)
-        return pltpu.make_async_copy(pieces1.at[at], pieces_out.at[at], pieces_sem.at[i])
 
     def receive(plane, pieces):
         kinetic = kinetic_of(lattice[...])
@@ -189,7 +189,9 @@
             @pl.when(k != n // 2)
             def _():
                 scale_copy(plane, k, d).wait()
-                code_copy(plane, k, d).wait()
+                code_copy(plane, k, d).wait_recv()
+                if plane == 1:
+                    code_copy(plane, k, d).wait_send()
 
             return 0
 
@@ -206,8 +208,6 @@
             at = pl.ds(pl.multiple_of(i * group * rows, group * rows), group * rows)
             pieces[at, : 2 * cols] = top
             pieces[at, 2 * cols :] = (both - top.astype(jnp.float32)).astype(jnp.bfloat16)
-            if plane == 1:
-                rows_copy(i).start()
 
         def in_turn(k, _):
             arrive(k, 0)
@@ -247,11 +247,13 @@
     lax.fori_loop(n // 2, n, functools.partial(send, 0), 0)
     loads[5].wait()
     loads[6].wait()
-    lax.fori_loop(0, n, functools.partial(send, 1), 0)
     for load in loads[7:]:
         load.wait()
 
+    lax.fori_loop(0, n // 2, functools.partial(send, 1), 0)
     for i in range(3):
+        if i == 1:
+            lax.fori_loop(n // 2, n, functools.partial(send, 1), 0)
         far_copy(i, fetched[i]).wait_recv()
         at = pl.ds(pl.multiple_of(own_start + fetched[i] * part, part), part)
         near = pl.ds(pl.multiple_of(fetched[i] * part, part), part)
@@ -266,14 +268,8 @@
     receive(0, pieces0)
     for i in range(PARTS):
         back_copy(i, other_start, fetched[i]).wait_recv()
-    stores = [
-        pltpu.make_async_copy(src, dst, store_sem.at[i])
-        for i, (src, dst) in enumerate(
-            ((vmat_ref, vmat_out), (psi_sum, psi0_out), (hpsi_sum, hpsi0_out))
-        )
-    ]
-    stores[0].start()
-
+    store = pltpu.make_async_copy(vmat_ref, vmat_out, store_sem)
+    store.start()
     def tile(j, _):
         at = pl.ds(pl.multiple_of(j * TILE, TILE), TILE)
         total = rotated(vmat_ref[:, at], pieces0[...])
@@ -282,8 +278,6 @@
         return 0
 
     lax.fori_loop(0, vmat_ref.shape[1] // TILE, tile, 0)
-    stores[1].start()
-    stores[2].start()
 
     receive(1, pieces1)
     for i in range(3):
@@ -291,10 +285,7 @@
         far_copy(i, fetched[i]).wait_send()
     for i in range(PARTS):
         back_copy(i, own_start, fetched[i]).wait_send()
-    for store in stores:
-        store.wait()
-    for i in range(n // group):
-        rows_copy(i).wait()
+    store.wait()
 
 
 def exchange(n, keepers, res, loc, store, lattice, psi, hpsi):
@@ -310,18 +301,16 @@
     return pl.pallas_call(
         functools.partial(exchange_kernel, n, rows, chunks),
         out_shape=(
-            jax.ShapeDtypeStruct((depth, span), jnp.bfloat16), parts, plane, plane,
+            jax.ShapeDtypeStruct((depth, span), jnp.bfloat16), parts, plane, plane, plane, plane,
         ),
         in_specs=[hbm] * 7,
-        out_specs=(hbm,) * 4,
+        out_specs=(hbm,) + (pl.BlockSpec(memory_space=pltpu.VMEM),) * 5,
         scratch_shapes=[
             pltpu.SMEM((2,), jnp.int32),
             pltpu.VMEM(flat, jnp.float32),
             pltpu.VMEM(flat, jnp.float32),
             pltpu.VMEM((depth, span), jnp.bfloat16),
             pltpu.VMEM(lattice.shape, jnp.int32),
-            pltpu.VMEM((span, cols), jnp.bfloat16),
-            pltpu.VMEM((span, cols), jnp.bfloat16),
             pltpu.VMEM((depth, span), jnp.bfloat16),
             pltpu.VMEM((planes, n, 2 * rows, cols), jnp.int16),
             pltpu.VMEM((planes, n, 8, cols), jnp.float32),
@@ -330,8 +319,7 @@
             pltpu.VMEM((depth // 2, span), jnp.bfloat16),
             pltpu.VMEM((depth // 2, span), jnp.bfloat16),
             pltpu.VMEM((depth, 4 * cols), jnp.bfloat16),
-            pltpu.VMEM((depth, 4 * cols), jnp.bfloat16),
-            dma((10,)), dma((3,)), dma((n,)), dma((planes, n)), dma((planes, n)), dma((planes, n)), dma((planes, n)),
+            dma((12,)), dma, dma((planes, n)), dma((planes, n)), dma((planes, n)), dma((planes, n)),
             dma((3,)), dma((3,)), dma((3,)), dma((3,)), dma, dma,
             dma((PARTS,)), dma((PARTS,)),
         ],
@@ -345,74 +333,43 @@
 
 
 def rotate_kernel(
-    vmat_hbm, pieces_hbm, psi0_hbm, hpsi0_hbm, psi_hbm, hpsi_hbm,
-    psi_out, hpsi_out,
-    vmat, pieces, psi, hpsi, psi0, hpsi0,
-    pieces_sem, vmat_sem, psi_sem, hpsi_sem, psi_out_sem, hpsi_out_sem, first_sem, first_out_sem,
+    vmat_hbm, pieces, psi0, hpsi0, psi1, hpsi1, psi_out, hpsi_out,
+    vmat, psi, hpsi, vmat_sem, psi_sem, hpsi_sem, first_sem,
 ):
     span, cols = psi.shape
     tiles = span // TILE
-
-    def tile(j):
-        return pl.ds(pl.multiple_of(j * TILE, TILE), TILE)
-
-    def loads(j):
-        at = tile(j)
-        return (
-            pltpu.make_async_copy(vmat_hbm.at[:, at], vmat.at[:, at], vmat_sem.at[j]),
-            pltpu.make_async_copy(psi_hbm.at[1, at], psi.at[at], psi_sem.at[j]),
-            pltpu.make_async_copy(hpsi_hbm.at[1, at], hpsi.at[at], hpsi_sem.at[j]),
-        )
-
-    def stores(j):
-        at = tile(j)
-        return (
-            pltpu.make_async_copy(psi.at[at], psi_out.at[1, at], psi_out_sem.at[j]),
-            pltpu.make_async_copy(hpsi.at[at], hpsi_out.at[1, at], hpsi_out_sem.at[j]),
-        )
-
-    load_pieces = pltpu.make_async_copy(pieces_hbm, pieces, pieces_sem)
-    first_in = (
-        pltpu.make_async_copy(psi0_hbm, psi0, first_sem.at[0]),
-        pltpu.make_async_copy(hpsi0_hbm, hpsi0, first_sem.at[1]),
+    first = (
+        pltpu.make_async_copy(psi0, psi_out.at[0], first_sem.at[0]),
+        pltpu.make_async_copy(hpsi0, hpsi_out.at[0], first_sem.at[1]),
     )
-    first_out = (
-        pltpu.make_async_copy(psi0, psi_out.at[0], first_out_sem.at[0]),
-        pltpu.make_async_copy(hpsi0, hpsi_out.at[0], first_out_sem.at[1]),
-    )
-    load_pieces.start()
-    for load in loads(0) + loads(1):
-        load.start()
-    for load in first_in:
-        load.start()
-    for j in range(2, tiles):
-        for load in loads(j):
-            load.start()
-    load_pieces.wait()
-
+    loads = []
     for j in range(tiles):
-        for load in loads(j):
-            load.wait()
-        at = tile(j)
+        at = pl.ds(j * TILE, TILE)
+        loads.append(pltpu.make_async_copy(vmat_hbm.at[:, at], vmat.at[:, at], vmat_sem.at[j]))
+        loads[-1].start()
+    for store in first:
+        store.start()
+    stores = []
+    for j in range(tiles):
+        at = pl.ds(j * TILE, TILE)
+        loads[j].wait()
         total = rotated(vmat[:, at], pieces[...])
-        psi[at, :] = (psi[at, :].astype(jnp.float32) + total[:, :cols]).astype(jnp.bfloat16)
-        hpsi[at, :] = (hpsi[at, :].astype(jnp.float32) + total[:, cols:]).astype(jnp.bfloat16)
-        for store in stores(j):
+        psi[at, :] = (psi1[at, :].astype(jnp.float32) + total[:, :cols]).astype(jnp.bfloat16)
+        hpsi[at, :] = (hpsi1[at, :].astype(jnp.float32) + total[:, cols:]).astype(jnp.bfloat16)
+        stores += [
+            pltpu.make_async_copy(psi.at[at], psi_out.at[1, at], psi_sem.at[j]),
+            pltpu.make_async_copy(hpsi.at[at], hpsi_out.at[1, at], hpsi_sem.at[j]),
+        ]
+        for store in stores[-2:]:
             store.start()
-        if j == 0:
-            for i in range(2):
-                first_in[i].wait()
-                first_out[i].start()
-    for j in range(tiles):
-        for store in stores(j):
-            store.wait()
-    for store in first_out:
+    for store in stores:
         store.wait()
-
-
-def rotate(vmat, pieces, psi0, hpsi0, psi, hpsi):
-    depth, span = vmat.shape
-    cols = psi0.shape[1]
+    for store in first:
+        store.wait()
+
+
+def rotate(vmat, pieces, psi0, hpsi0, psi1, hpsi1):
+    span, cols = psi0.shape
     tiles = span // TILE
     dma = pltpu.SemaphoreType.DMA
     hbm = pl.BlockSpec(memory_space=pltpu.HBM)
@@ -421,26 +378,21 @@
     return pl.pallas_call(
         rotate_kernel,
         out_shape=(out, out),
-        in_specs=[hbm] * 6,
+        in_specs=[hbm] + [pl.BlockSpec(memory_space=pltpu.VMEM)] * 5,
         out_specs=(hbm, hbm),
         scratch_shapes=[
-            pltpu.VMEM((depth, span), jnp.bfloat16),
-            pltpu.VMEM((depth, 4 * cols), jnp.bfloat16),
-            plane, plane, plane, plane,
-            dma, dma((tiles,)), dma((tiles,)), dma((tiles,)), dma((tiles,)), dma((tiles,)),
-            dma((2,)), dma((2,)),
+            pltpu.VMEM(vmat.shape, vmat.dtype), plane, plane,
+            dma((tiles,)), dma((tiles,)), dma((tiles,)), dma((2,)),
         ],
         compiler_params=pltpu.CompilerParams(vmem_limit_bytes=GRANT),
-    )(vmat, pieces, psi0, hpsi0, psi, hpsi)
+    )(vmat, pieces, psi0, hpsi0, psi1, hpsi1)
 
 
 def per_device(n, res, loc, psi, hpsi, store, keepers, lattice):
     planes, span, _, cols = psi.shape
     psi_in, hpsi_in = (x.reshape(planes, span, cols) for x in (psi, hpsi))
-    vmat, pieces, psi0, hpsi0 = exchange(
-        n, keepers, res, loc, store, lattice, psi_in, hpsi_in
-    )
-    psi_new, hpsi_new = rotate(vmat, pieces, psi0, hpsi0, psi_in, hpsi_in)
+    handed = exchange(n, keepers, res, loc, store, lattice, psi_in, hpsi_in)
+    psi_new, hpsi_new = rotate(*handed)
     return psi_new.reshape(psi.shape), hpsi_new.reshape(hpsi.shape)
 
 

time: 41.6 us -> 46.5 us (1.12)
  the two profiles are of different devices: /device:TPU:0 before, /device:TPU:23 now
where the time goes in v6:
time: 46.5 us; the launch traced here: 46.3 us
  Pallas kernels  44.4 us (95%)
  local copies, waits for them, and re-layouts  1.33 us (3%)
  between operations  0.65 us (1%)
    pallas_call x1, Pallas kernels, exchange(): pl.pallas_call(functools.partial(exchange_kernel, n, rows, chunks), out_s...  36.9 us
    pallas_call x1, Pallas kernels, rotate(): pl.pallas_call(rotate_kernel, out_shape=(out, out), in_specs=[hbm] + [pl....  7.49 us
    unnamed x4, local copies, waits for them, and re-layouts  1.33 us

profile of v6, /device:TPU:23, one launch (start us, length us, event | category | flops | bytes accessed | tf_op | source)
XLA Modules:
  0.0 46.3 jit_solution(11234376102395873176)
XLA Ops:
  0.6 0.0 copy-start
  0.6 0.7 %copy-done = s32[1,256]{1,0:T(1,128)S(1)} copy-done((s32[1,256]{1,0:T(1,128)S(1)}, s32[1,256]{1,0:T(1,128)}, u32[]{:S(2)}) %copy-start) | copy-done | bytes 1048
  1.3 0.0 copy-start.1
  1.3 0.7 %copy-done.1 = s32[2]{0:T(128)S(1)} copy-done((s32[2]{0:T(128)S(1)}, s32[2]{0:T(128)}, u32[]{:S(2)}) %copy-start.1) | copy-done | bytes 32
  2.0 36.9 %shard_map.86 = (bf16[512,2048]{1,0:T(8,128)(2,1)}, bf16[512,1024]{1,0:T(8,128)(2,1)S(1)}, bf16[2048,256]{1,0:T(8,128)(2,1)}, bf16[2048,256]{1,0:T(8,128)(2,1)},...) custom-call(s32[2]{0:T(128)S(1)} %copy-done.1, f32[2048,128]{1,0:T(8,128)} %bitcast.14, f32[2048,128]{1,0:T(8,128)} %bitcast.15, ...), custom_call_target="tpu_custom_call" | custom-call | tf_op jit(solution)/shard_map/pallas_call | solution.py:301
  38.9 7.5 %shard_map.87 = (bf16[2,2048,256]{2,1,0:T(8,128)(2,1)}, bf16[2,2048,256]{2,1,0:T(8,128)(2,1)}) custom-call(bf16[512,2048]{1,0:T(8,128)(2,1)} %get-tuple-element.10.vmat_hbm, bf16[512,1024]{1,0:T(8,128)(2,1)S(1)} %get-tuple-element.11.pieces, bf16[2048,256]{1,0:T(8,128)(2,1)} %get-tuple-element.12.psi0, bf16[2048,256]{1,0:T(8,128)(2,1)} %get-tuple-element.13.hpsi0, ...), custom_call_target="tpu_custom_call" | custom-call | tf_op jit(solution)/shard_map/pallas_call | solution.py:378
Async XLA Ops:
  0.6 0.7 %copy-start = (s32[1,256]{1,0:T(1,128)S(1)}, s32[1,256]{1,0:T(1,128)}, u32[]{:S(2)}) copy-start(s32[1,256]{1,0:T(1,128)} %lattice_hbm.1) | copy-start | bytes 3076
  1.3 0.7 %copy-start.1 = (s32[2]{0:T(128)S(1)}, s32[2]{0:T(128)}, u32[]{:S(2)}) copy-start(s32[2]{0:T(128)} %keepers_hbm.1) | copy-start | bytes 28

commit v7 on v6

--- a/solution.py
+++ b/solution.py
@@ -12,7 +12,7 @@
 PARTS = 4
 TOP = 32766.0
 TILE = 512
-GRANT = 52 * 2**20
+GRANT = 48 * 2**20
 MESH = pl.DeviceIdType.MESH
 
 
@@ -171,8 +171,6 @@
 
         @pl.when(k != n // 2)
         def _():
-            if plane == 1:
-                code_copy(0, k, d).wait_send()
             scale_copy(plane, k, d).start()
             code_copy(plane, k, d).start()
 
@@ -189,9 +187,7 @@
             @pl.when(k != n // 2)
             def _():
                 scale_copy(plane, k, d).wait()
-                code_copy(plane, k, d).wait_recv()
-                if plane == 1:
-                    code_copy(plane, k, d).wait_send()
+                code_copy(plane, k, d).wait()
 
             return 0
 
@@ -247,13 +243,11 @@
     lax.fori_loop(n // 2, n, functools.partial(send, 0), 0)
     loads[5].wait()
     loads[6].wait()
+    lax.fori_loop(0, n, functools.partial(send, 1), 0)
     for load in loads[7:]:
         load.wait()
 
-    lax.fori_loop(0, n // 2, functools.partial(send, 1), 0)
     for i in range(3):
-        if i == 1:
-            lax.fori_loop(n // 2, n, functools.partial(send, 1), 0)
         far_copy(i, fetched[i]).wait_recv()
         at = pl.ds(pl.multiple_of(own_start + fetched[i] * part, part), part)
         near = pl.ds(pl.multiple_of(fetched[i] * part, part), part)

time: 46.5 us -> 41 us (0.88)
  the two profiles are of different devices: /device:TPU:23 before, /device:TPU:0 now
where the time goes in v7:
time: 41 us; the launch traced here: 40.8 us
  Pallas kernels  38.9 us (95%)
  local copies, waits for them, and re-layouts  1.33 us (3%)
  between operations  0.65 us (2%)
    pallas_call x1, Pallas kernels, exchange(): pl.pallas_call(functools.partial(exchange_kernel, n, rows, chunks), out_s...  33.5 us
    pallas_call x1, Pallas kernels, rotate(): pl.pallas_call(rotate_kernel, out_shape=(out, out), in_specs=[hbm] + [pl....  5.32 us
    unnamed x4, local copies, waits for them, and re-layouts  1.33 us

profile of v7, /device:TPU:0, one launch (start us, length us, event | category | flops | bytes accessed | tf_op | source)
XLA Modules:
  0.0 40.8 jit_solution(8626621550448126714)
XLA Ops:
  0.6 0.0 copy-start
  0.6 0.7 %copy-done = s32[1,256]{1,0:T(1,128)S(1)} copy-done((s32[1,256]{1,0:T(1,128)S(1)}, s32[1,256]{1,0:T(1,128)}, u32[]{:S(2)}) %copy-start) | copy-done | bytes 1048
  1.3 0.0 copy-start.1
  1.3 0.7 %copy-done.1 = s32[2]{0:T(128)S(1)} copy-done((s32[2]{0:T(128)S(1)}, s32[2]{0:T(128)}, u32[]{:S(2)}) %copy-start.1) | copy-done | bytes 32
  2.0 33.5 %shard_map.86 = (bf16[512,2048]{1,0:T(8,128)(2,1)}, bf16[512,1024]{1,0:T(8,128)(2,1)S(1)}, bf16[2048,256]{1,0:T(8,128)(2,1)S(1)}, bf16[2048,256]{1,0:T(8,128)(2,...) custom-call(s32[2]{0:T(128)S(1)} %copy-done.1, f32[2048,128]{1,0:T(8,128)} %bitcast.14, ...), custom_call_target="tpu_custom_call" | custom-call | tf_op jit(solution)/shard_map/pallas_call | solution.py:295
  35.5 5.3 %shard_map.87 = (bf16[2,2048,256]{2,1,0:T(8,128)(2,1)}, bf16[2,2048,256]{2,1,0:T(8,128)(2,1)}) custom-call(bf16[512,2048]{1,0:T(8,128)(2,1)} %get-tuple-element.10.vmat_hbm, bf16[512,1024]{1,0:T(8,128)(2,1)S(1)} %get-tuple-element.11.pieces, bf16[2048,256]{1,0:T(8,128)(2,1)S(1)} %get-tuple-element.12.psi0, bf16[2048,256]{1,0:T(8,128)(2,1)S(1)} %get-tuple-element.13.hpsi0, ...), custom_call_target="tpu_custom_call" | custom-call | tf_op jit(solution)/shard_map/pallas_call | solution.py:372
Async XLA Ops:
  0.6 0.7 %copy-start = (s32[1,256]{1,0:T(1,128)S(1)}, s32[1,256]{1,0:T(1,128)}, u32[]{:S(2)}) copy-start(s32[1,256]{1,0:T(1,128)} %lattice_hbm.1) | copy-start | bytes 3076
  1.3 0.7 %copy-start.1 = (s32[2]{0:T(128)S(1)}, s32[2]{0:T(128)}, u32[]{:S(2)}) copy-start(s32[2]{0:T(128)} %keepers_hbm.1) | copy-start | bytes 28

commit v8 on v7

--- a/solution.py
+++ b/solution.py
@@ -36,9 +36,9 @@
 
 def exchange_kernel(
     n, rows, chunks,
-    keepers_hbm, res_hbm, loc_hbm, store_hbm, lattice_hbm, psi_hbm, hpsi_hbm,
+    lattice_hbm, res_hbm, loc_hbm, store_hbm, psi_hbm, hpsi_hbm,
     vmat_out, pieces1, psi_sum, hpsi_sum, psi1, hpsi1,
-    keepers, res, loc, masked, lattice, vmat_ref,
+    lattice, res, loc, masked, vmat_ref,
     out_codes, out_scales, codes, scales, chip_sum, far_sum, pieces0,
     load_sem, store_sem, code_send, code_recv, scale_send, scale_recv,
     sib_send, sib_recv, far_send, far_recv, side_send, side_recv, back_send, back_recv,
@@ -65,14 +65,13 @@
         pltpu.make_async_copy(src, dst, load_sem.at[i])
         for i, (src, dst) in enumerate(
             (
-                (keepers_hbm, keepers),
+                (lattice_hbm, lattice),
                 (store_hbm.at[other], masked.at[other]),
                 (res_hbm.at[first], res.at[first]),
                 (loc_hbm.at[first], loc.at[first]),
                 (store_hbm.at[mine], masked.at[mine]),
                 (res_hbm.at[second], res.at[second]),
                 (loc_hbm.at[second], loc.at[second]),
-                (lattice_hbm, lattice),
                 (psi_hbm.at[0], psi_sum),
                 (hpsi_hbm.at[0], hpsi_sum),
                 (psi_hbm.at[1], psi1),
@@ -179,7 +178,7 @@
     group = max(1, 16 // rows)
 
     def receive(plane, pieces):
-        kinetic = kinetic_of(lattice[...])
+        kinetic = kinetic_of(lattice[0:1, :])
 
         def arrive(k, _):
             d = (me + n // 2 + k) % n
@@ -221,7 +220,7 @@
             lax.fori_loop(0, n // group, in_order, 0)
 
     def keep(panel):
-        return (keepers[panel] == band).astype(jnp.float32).astype(jnp.bfloat16)
+        return (lattice[pl.ds(1 + panel, 1), :][:, :1] == band).astype(jnp.float32).astype(jnp.bfloat16)
 
     loads[0].wait()
     loads[1].wait()
@@ -297,14 +296,13 @@
         out_shape=(
             jax.ShapeDtypeStruct((depth, span), jnp.bfloat16), parts, plane, plane, plane, plane,
         ),
-        in_specs=[hbm] * 7,
+        in_specs=[hbm] * 6,
         out_specs=(hbm,) + (pl.BlockSpec(memory_space=pltpu.VMEM),) * 5,
         scratch_shapes=[
-            pltpu.SMEM((2,), jnp.int32),
+            pltpu.VMEM((3, cols), jnp.int32),
             pltpu.VMEM(flat, jnp.float32),
             pltpu.VMEM(flat, jnp.float32),
             pltpu.VMEM((depth, span), jnp.bfloat16),
-            pltpu.VMEM(lattice.shape, jnp.int32),
             pltpu.VMEM((depth, span), jnp.bfloat16),
             pltpu.VMEM((planes, n, 2 * rows, cols), jnp.int16),
             pltpu.VMEM((planes, n, 8, cols), jnp.float32),
@@ -313,7 +311,7 @@
             pltpu.VMEM((depth // 2, span), jnp.bfloat16),
             pltpu.VMEM((depth // 2, span), jnp.bfloat16),
             pltpu.VMEM((depth, 4 * cols), jnp.bfloat16),
-            dma((12,)), dma, dma((planes, n)), dma((planes, n)), dma((planes, n)), dma((planes, n)),
+            dma((11,)), dma, dma((planes, n)), dma((planes, n)), dma((planes, n)), dma((planes, n)),
             dma((3,)), dma((3,)), dma((3,)), dma((3,)), dma, dma,
             dma((PARTS,)), dma((PARTS,)),
         ],
@@ -321,8 +319,8 @@
             collective_id=0, has_side_effects=True, vmem_limit_bytes=GRANT
         ),
     )(
-        keepers, res.reshape(flat), loc.reshape(flat), store.reshape(depth, span),
-        lattice, psi, hpsi,
+        jnp.concatenate([lattice, jnp.broadcast_to(keepers[:, None], (2, cols))], axis=0),
+        res.reshape(flat), loc.reshape(flat), store.reshape(depth, span), psi, hpsi,
     )
 
 

time: 41 us -> 41.2 us (level)
  other arithmetic: 0 us -> 0.75 us
  local copies, waits for them, and re-layouts: 1.33 us -> 0.73 us
    unnamed x4 -> x0, local copies, waits for them, and re-layouts: 1.33 us -> none
    concatenate x0 -> x1, other arithmetic: none -> 0.75 us  [exchange(): jnp.concatenate([lattice, jnp.broadcast_to(keepers[:, None], (2, cols))],...]
    concatenate x0 -> x1, local copies, waits for them, and re-layouts: none -> 0.73 us  [exchange(): jnp.concatenate([lattice, jnp.broadcast_to(keepers[:, None], (2, cols))],...]
where the time goes in v8:
time: 41.2 us; the launch traced here: 41 us
  Pallas kernels  38.9 us (94%)
  other arithmetic  0.75 us (2%)
  local copies, waits for them, and re-layouts  0.73 us (2%)
  between operations  0.64 us (2%)
    pallas_call x1, Pallas kernels, exchange(): pl.pallas_call(functools.partial(exchange_kernel, n, rows, chunks), out_s...  33.6 us
    pallas_call x1, Pallas kernels, rotate(): pl.pallas_call(rotate_kernel, out_shape=(out, out), in_specs=[hbm] + [pl....  5.34 us

profile of v8, /device:TPU:0, one launch (start us, length us, event | category | flops | bytes accessed | tf_op | source)
XLA Modules:
  0.0 41.0 jit_solution(8354381457486296887)
XLA Ops:
  0.6 0.7 %pad.1.clone = s32[3]{0:T(128)S(1)} pad(s32[2]{0:T(128)} %param.12, s32[]{:T(128)} %constant.6), padding=1_0 | pad | bytes 24 | tf_op jit(solution)/shard_map/concatenate | solution.py:322
  1.4 0.7 %pad_add_fusion.lattice_hbm = s32[3,256]{1,0:T(4,128)S(1)} fusion(s32[1,256]{1,0:T(1,128)} %param.13, s32[3]{0:T(128)S(1)} %pad.1.clone), kind=kLoop, calls=%fused_computation | loop fusion | flops 768 | bytes 4108 | tf_op jit(solution)/shard_map/concatenate | solution.py:322
  2.1 33.6 %shard_map.86 = (bf16[512,2048]{1,0:T(8,128)(2,1)}, bf16[512,1024]{1,0:T(8,128)(2,1)S(1)}, bf16[2048,256]{1,0:T(8,128)(2,1)S(1)}, bf16[2048,256]{1,0:T(8,128)(2,...) custom-call(s32[3,256]{1,0:T(4,128)S(1)} %pad_add_fusion.lattice_hbm, f32[2048,128]{1,0:T(8,128)} %bitcast.14, ...), custom_call_target="tpu_custom_call" | custom-call | tf_op jit(solution)/shard_map/pallas_call | solution.py:294
  35.7 5.3 %shard_map.87 = (bf16[2,2048,256]{2,1,0:T(8,128)(2,1)}, bf16[2,2048,256]{2,1,0:T(8,128)(2,1)}) custom-call(bf16[512,2048]{1,0:T(8,128)(2,1)} %get-tuple-element.10.vmat_hbm, bf16[512,1024]{1,0:T(8,128)(2,1)S(1)} %get-tuple-element.11.pieces, bf16[2048,256]{1,0:T(8,128)(2,1)S(1)} %get-tuple-element.12.psi0, bf16[2048,256]{1,0:T(8,128)(2,1)S(1)} %get-tuple-element.13.hpsi0, ...), custom_call_target="tpu_custom_call" | custom-call | tf_op jit(solution)/shard_map/pallas_call | solution.py:370
